TPU v7x, 32 devices: a whole 2x2x4 slice. The times are simulated.
32 devices in a mesh: section: 2 (over x), dp: 16 (over z, y, core).
Axes of the slice: x: 2, y: 2, z: 4, core: 2. Of those that a mesh axis runs over, the one named last changes fastest.
Arguments:
- inputs: bfloat16 [24448, 384], P('dp'), may hold values from -6 to 6
- cotangent: bfloat16 [24448, 384], P('dp'), may hold values from -6 to 6
- wide_weights: float32 [2, 384, 2688], P('section', 'dp'), may hold values from -0.3125 to 0.3125
- wide_first: float32 [2, 384, 2688], P('section', 'dp'), may hold values from -469.07569 to 469.07569
- wide_second: float32 [2, 384, 2688], P('section', 'dp'), may hold values from 0 to 48896
- tall_weights: float32 [2, 1920, 384], P('section', 'dp'), as said below
- tall_first: float32 [2, 1920, 384], P('section', 'dp'), may hold values from -469.07569 to 469.07569
- tall_second: float32 [2, 1920, 384], P('section', 'dp'), may hold values from 0 to 48896
- vectors: float32 [2, 12, 384], P('section', None, 'dp'), as said below
- vector_first: float32 [2, 12, 384], P('section', None, 'dp'), may hold values from -469.07569 to 469.07569
- vector_second: float32 [2, 12, 384], P('section', None, 'dp'), may hold values from 0 to 48896
Outputs:
- activations: bfloat16 [2, 24448, 384], P('section', 'dp')
- input_grads: bfloat16 [2, 24448, 384], P('section', 'dp')
- new_wide_first: float32 [2, 384, 2688], P('section', 'dp')
- new_wide_second: float32 [2, 384, 2688], P('section', 'dp')
- new_wide_weights: float32 [2, 384, 2688], P('section', 'dp')
- new_tall_first: float32 [2, 1920, 384], P('section', 'dp')
- new_tall_second: float32 [2, 1920, 384], P('section', 'dp')
- new_tall_weights: float32 [2, 1920, 384], P('section', 'dp')
- new_vector_first: float32 [2, 12, 384], P('section', None, 'dp')
- new_vector_second: float32 [2, 12, 384], P('section', None, 'dp')
- new_vectors: float32 [2, 12, 384], P('section', None, 'dp')
Inputs may be any that keep to these rules, and one draw needn't show every extreme that they name: `tall_weights`: rows below 384 of each layer are about 4 / sqrt(384) in spread, the rest about 1.5 / sqrt(1536). `vectors`: rows 0 and 5 of each layer are gains near 1; the others are biases.
All inputs are finite; a program needn't handle non-finite values.
Results may differ from a plain program's by a relative error of at most 0.014.
Values may be sent and summed in bfloat16 or wider, within the bound.
A program may use at most 192 MiB of HBM per device.

v0:
```python
import jax
import jax.numpy as jnp
from jax import lax
from jax.sharding import PartitionSpec as P

HEADS = 6
HEAD_DIM = 64
GLOBAL = 2
GLOBAL_LEN = 197
LOCAL = 10
LOCAL_LEN = 37
STEP = 5


NORM_EPS = 1e-06
BETA_ONE = 0.5
BETA_TWO = 0.5
ADAM_EPS = 1e-08
RATE_MATRIX = 0.05
RATE_VECTOR = 0.2
DECAY = 0.05
ERF_SCALE = 0.7071067811865476
DENSITY_SCALE = 0.3989422804014327


def from_behind(value, axis, steps):
    count = lax.axis_size(axis)
    initial, last = (max(0, -steps), min(count, count - steps))
    return lax.ppermute(value, axis, [(source, source + steps) for source in range(initial, last)])


def product(former, latter):
    return jnp.dot(former, latter, preferred_element_type=jnp.float32)


def inner(former, latter):
    return lax.dot_general(
        former, latter, (((0,), (0,)), ((), ())), preferred_element_type=jnp.float32
    )


def outer(former, latter):
    return lax.dot_general(
        former, latter, (((1,), (1,)), ((), ())), preferred_element_type=jnp.float32
    )


def standard(values):
    centre = values - jnp.mean(values, axis=-1, keepdims=True)
    inverse = lax.rsqrt(jnp.mean(centre * centre, axis=-1, keepdims=True) + NORM_EPS)
    return (centre * inverse, inverse)


def norm_back(normed, inverse, gain_row, incoming):
    scaled = incoming * gain_row
    result = inverse * (
        scaled
        - jnp.mean(scaled, axis=-1, keepdims=True)
        - normed * jnp.mean(scaled * normed, axis=-1, keepdims=True)
    )
    return (result, jnp.sum(incoming * normed, axis=0), jnp.sum(incoming, axis=0))


def gelu_value(values):
    return 0.5 * values * (1.0 + lax.erf(values * ERF_SCALE))


def gelu_slope(values):
    return (
        0.5 * (1.0 + lax.erf(values * ERF_SCALE))
        + values * jnp.exp(-0.5 * values * values) * DENSITY_SCALE
    )


def attend(packed, crop_count, length):
    by_head = packed.reshape(crop_count, length, 3, HEADS, HEAD_DIM)
    queries = by_head[:, :, 0]
    key_rows = by_head[:, :, 1]
    value_rows = by_head[:, :, 2]
    scores = jnp.einsum(
        "cqhd,ckhd->chqk", queries, key_rows, preferred_element_type=jnp.float32
    ) * HEAD_DIM ** (-0.5)
    largest = jnp.max(scores, axis=-1, keepdims=True)
    exponent = jnp.exp(scores - largest)
    summed = jnp.sum(exponent, axis=-1, keepdims=True)
    weights = (exponent / summed).astype(jnp.bfloat16)
    mixture = jnp.einsum("chqk,ckhd->cqhd", weights, value_rows, preferred_element_type=jnp.float32)
    return (mixture.reshape(crop_count * length, HEADS * HEAD_DIM), largest + jnp.log(summed))


def attention_back(packed, largest_log, grad_out, crop_count, length):
    by_head = packed.reshape(crop_count, length, 3, HEADS, HEAD_DIM)
    queries = by_head[:, :, 0]
    key_rows = by_head[:, :, 1]
    value_rows = by_head[:, :, 2]
    factor = HEAD_DIM ** (-0.5)
    scores = (
        jnp.einsum("cqhd,ckhd->chqk", queries, key_rows, preferred_element_type=jnp.float32)
        * factor
    )
    weights = jnp.exp(scores - largest_log)
    grad_heads = grad_out.reshape(crop_count, length, HEADS, HEAD_DIM)
    grad_values = jnp.einsum(
        "chqk,cqhd->ckhd",
        weights.astype(jnp.bfloat16),
        grad_heads,
        preferred_element_type=jnp.float32,
    )
    grad_weights = jnp.einsum(
        "cqhd,ckhd->chqk", grad_heads, value_rows, preferred_element_type=jnp.float32
    )
    grad_scores = (
        weights * (grad_weights - jnp.sum(grad_weights * weights, axis=-1, keepdims=True))
    ).astype(jnp.bfloat16)
    grad_queries = (
        jnp.einsum("chqk,ckhd->cqhd", grad_scores, key_rows, preferred_element_type=jnp.float32)
        * factor
    )
    grad_keys = (
        jnp.einsum("chqk,cqhd->ckhd", grad_scores, queries, preferred_element_type=jnp.float32)
        * factor
    )
    stacked = jnp.stack((grad_queries, grad_keys, grad_values), axis=2)
    return stacked.reshape(crop_count * length, 3 * HEADS * HEAD_DIM)


def forward(tokens, w_qkv, w_proj, w_up, w_down, gains):
    global_rows = GLOBAL * GLOBAL_LEN
    current = tokens.astype(jnp.float32)
    normed_one, inverse_one = standard(current)
    mix_input = (normed_one * gains[0] + gains[1]).astype(jnp.bfloat16)
    bias_row = jnp.concatenate((gains[2], jnp.zeros_like(gains[2]), gains[3]))
    packed = (product(mix_input, w_qkv) + bias_row).astype(jnp.bfloat16)
    global_mix, global_log = attend(packed[:global_rows], GLOBAL, GLOBAL_LEN)
    local_mix, local_log = attend(packed[global_rows:], LOCAL, LOCAL_LEN)
    mixture = jnp.concatenate((global_mix, local_mix)).astype(jnp.bfloat16)
    hidden = current + product(mixture, w_proj) + gains[4]
    normed_two, inverse_two = standard(hidden)
    feed_input = (normed_two * gains[5] + gains[6]).astype(jnp.bfloat16)
    pre_gelu = product(feed_input, w_up) + gains[8:].reshape(-1)
    activated = gelu_value(pre_gelu).astype(jnp.bfloat16)
    output = hidden + product(activated, w_down) + gains[7]
    kept = (
        normed_one,
        inverse_one,
        mix_input,
        packed,
        global_log,
        local_log,
        mixture,
        normed_two,
        inverse_two,
        feed_input,
        pre_gelu,
        activated,
    )
    return (output, kept)


def backward(kept, grad_in, w_qkv, w_proj, w_up, w_down, gains):
    (
        normed_one,
        inverse_one,
        mix_input,
        packed,
        global_log,
        local_log,
        mixture,
        normed_two,
        inverse_two,
        feed_input,
        pre_gelu,
        activated,
    ) = kept
    global_rows = GLOBAL * GLOBAL_LEN
    width = w_proj.shape[1]
    grad_top = grad_in.astype(jnp.float32)
    grad_down = inner(activated, grad_in)
    grad_act = outer(grad_in, w_down)
    grad_pre = (grad_act * gelu_slope(pre_gelu)).astype(jnp.bfloat16)
    grad_up = inner(feed_input, grad_pre)
    grad_feed = outer(grad_pre, w_up)
    back_two, gain_two, shift_two = norm_back(normed_two, inverse_two, gains[5], grad_feed)
    grad_hidden = grad_top + back_two
    grad_branch = grad_hidden.astype(jnp.bfloat16)
    grad_proj = inner(mixture, grad_branch)
    grad_mix = outer(grad_branch, w_proj).astype(jnp.bfloat16)
    global_part = attention_back(
        packed[:global_rows], global_log, grad_mix[:global_rows], GLOBAL, GLOBAL_LEN
    )
    local_part = attention_back(
        packed[global_rows:], local_log, grad_mix[global_rows:], LOCAL, LOCAL_LEN
    )
    grad_packed = jnp.concatenate((global_part, local_part)).astype(jnp.bfloat16)
    grad_qkv = inner(mix_input, grad_packed)
    grad_norm = outer(grad_packed, w_qkv)
    back_one, gain_one, shift_one = norm_back(normed_one, inverse_one, gains[0], grad_norm)
    grad_tokens = grad_hidden + back_one
    packed_sums = jnp.sum(grad_packed, axis=0, dtype=jnp.float32)
    leading = jnp.stack(
        (
            gain_one,
            shift_one,
            packed_sums[:width],
            packed_sums[2 * width :],
            jnp.sum(grad_branch, axis=0, dtype=jnp.float32),
            gain_two,
            shift_two,
            jnp.sum(grad_top, axis=0),
        )
    )
    up_bias = jnp.sum(grad_pre, axis=0, dtype=jnp.float32).reshape(-1, width)
    vector_grads = jnp.concatenate((leading, up_bias), axis=0)
    return (
        grad_tokens,
        jnp.concatenate((grad_qkv, grad_up), axis=1),
        jnp.concatenate((grad_proj, grad_down), axis=0),
        vector_grads,
    )


def adamw(weights, first, second, grads, rate, decay):
    first_new = BETA_ONE * first + (1.0 - BETA_ONE) * grads
    second_new = BETA_TWO * second + (1.0 - BETA_TWO) * grads * grads
    corrected = (
        first_new
        / (1.0 - BETA_ONE**STEP)
        / (jnp.sqrt(second_new / (1.0 - BETA_TWO**STEP)) + ADAM_EPS)
    )
    return (first_new, second_new, weights - rate * (corrected + decay * weights))


def per_device(
    inputs,
    cotangent,
    wide_weights,
    wide_first,
    wide_second,
    tall_weights,
    tall_first,
    tall_second,
    vectors,
    vector_first,
    vector_second,
):
    section = lax.axis_index("section")
    wide_copy, tall_copy, vector_copy = (
        lax.all_gather(wide_weights[0].astype(jnp.bfloat16), "dp", axis=0, tiled=True),
        lax.all_gather(tall_weights[0].astype(jnp.bfloat16), "dp", axis=0, tiled=True),
        lax.all_gather(vectors[0].astype(jnp.bfloat16), "dp", axis=1, tiled=True),
    )
    width = tall_copy.shape[1]
    w_qkv = wide_copy[:, : 3 * width]
    w_up = wide_copy[:, 3 * width :]
    w_proj = tall_copy[:width]
    w_down = tall_copy[width:]
    gains = vector_copy.astype(jnp.float32)
    image_rows = GLOBAL * GLOBAL_LEN + LOCAL * LOCAL_LEN
    micro = inputs.shape[0] // image_rows
    empty_rows = jnp.zeros((image_rows, width), jnp.bfloat16)
    received = empty_rows
    outputs = []
    saved = []
    for tick_index in range(micro + 1):
        if tick_index < micro:
            own_rows = inputs[tick_index * image_rows : (tick_index + 1) * image_rows]
        else:
            own_rows = empty_rows
        current = jnp.where(section == 0, own_rows, received)
        result, kept = forward(current, w_qkv, w_proj, w_up, w_down, gains)
        sent = result.astype(jnp.bfloat16)
        outputs.append(sent)
        saved.append(kept)
        if tick_index < micro:
            received = from_behind(sent, "section", 1)
    totals = (
        jnp.zeros(wide_copy.shape, jnp.float32),
        jnp.zeros(tall_copy.shape, jnp.float32),
        jnp.zeros(vector_copy.shape, jnp.float32),
    )
    returned = empty_rows
    grads_in = []
    for tick_index in range(micro + 1):
        if tick_index < micro:
            own_rows = cotangent[
                (micro - 1 - tick_index) * image_rows : (micro - tick_index) * image_rows
            ]
        else:
            own_rows = empty_rows
        incoming = jnp.where(section == 1, own_rows, returned)
        grad_tokens, grad_wide, grad_tall, grad_vec = backward(
            saved[micro - tick_index], incoming, w_qkv, w_proj, w_up, w_down, gains
        )
        sent_back = grad_tokens.astype(jnp.bfloat16)
        grads_in.append(sent_back)
        if tick_index < micro:
            returned = from_behind(sent_back, "section", -1)
        totals = (totals[0] + grad_wide, totals[1] + grad_tall, totals[2] + grad_vec)
    totals = (
        lax.psum_scatter(totals[0], "dp", scatter_dimension=0, tiled=True),
        lax.psum_scatter(totals[1], "dp", scatter_dimension=0, tiled=True),
        lax.psum_scatter(totals[2], "dp", scatter_dimension=1, tiled=True),
    )
    activations = jnp.where(
        section == 0, jnp.concatenate(outputs[:micro]), jnp.concatenate(outputs[1:])
    )
    input_grads = jnp.where(
        section == 0, jnp.concatenate(grads_in[1:][::-1]), jnp.concatenate(grads_in[:micro][::-1])
    )
    wide_m, wide_s, wide_n = adamw(
        wide_weights[0], wide_first[0], wide_second[0], totals[0], RATE_MATRIX, DECAY
    )
    tall_m, tall_s, tall_n = adamw(
        tall_weights[0], tall_first[0], tall_second[0], totals[1], RATE_MATRIX, DECAY
    )
    vec_m, vec_s, vec_n = adamw(
        vectors[0], vector_first[0], vector_second[0], totals[2], RATE_VECTOR, 0.0
    )
    return (
        activations[None],
        input_grads[None],
        wide_m[None],
        wide_s[None],
        wide_n[None],
        tall_m[None],
        tall_s[None],
        tall_n[None],
        vec_m[None],
        vec_s[None],
        vec_n[None],
    )


def solution(mesh):
    in_specs = (
        P("dp", None),
        P("dp", None),
        P("section", "dp", None),
        P("section", "dp", None),
        P("section", "dp", None),
        P("section", "dp", None),
        P("section", "dp", None),
        P("section", "dp", None),
        P("section", None, "dp"),
        P("section", None, "dp"),
        P("section", None, "dp"),
    )
    out_specs = (
        P("section", "dp", None),
        P("section", "dp", None),
        P("section", "dp", None),
        P("section", "dp", None),
        P("section", "dp", None),
        P("section", "dp", None),
        P("section", "dp", None),
        P("section", "dp", None),
        P("section", None, "dp"),
        P("section", None, "dp"),
        P("section", None, "dp"),
    )
    return jax.shard_map(
        per_device, mesh=mesh, in_specs=in_specs, out_specs=out_specs, check_vma=False
    )
```

profile of v0, /device:TPU:0, one launch (start us, length us, event | category | flops | bytes accessed | tf_op | source)
XLA Modules:
  0.0 510.8 jit_solution(14146842564471840160)
XLA Ops:
  11.4 23.3 %all-gather = bf16[16,24,12]{1,2,0:T(8,128)(2,1)S(1)} all-gather(bf16[1,24,12]{1,2,0:T(8,128)(2,1)S(1)} %bitcast.363), channel_id=1, replica_groups=mesh['section'=2,'dp'=16] {'dp'}, dimensions={0}, use_global_device_ids=true | all-gather | bytes 9792 | tf_op jit(solution)/shard_map/all_gather | solution.py:250
  35.5 19.3 %all-gather.4.cloned.1.call-done = bf16[384,2688]{1,0:T(8,128)(2,1)} async-done(((bf16[24,2688]{1,0:T(8,128)(2,1)}), bf16[384,2688]{1,0:T(8,128)(2,1)}) %all-gather.4.cloned.1.call-update) | async-done | bytes 2064400 | tf_op jit(solution)/shard_map/all_gather | solution.py:248
  74.7 21.0 %all-gather.6.cloned.1.call-done = bf16[1920,384]{1,0:T(8,128)(2,1)} async-done(((bf16[120,384]{1,0:T(8,128)(2,1)}), bf16[1920,384]{1,0:T(8,128)(2,1)}) %all-gather.6.cloned.1.call-update) | async-done | bytes 1474576 | tf_op jit(solution)/shard_map/all_gather | solution.py:249
  102.8 3.9 collective-permute-start
  106.8 12.5 %collective-permute-done = bf16[764,384]{1,0:T(8,128)(2,1)S(1)} collective-permute-done((bf16[764,384]{1,0:T(8,128)(2,1)S(1)}, bf16[764,384]{1,0:T(8,128)(2,1)S(1)}, u32[]{:S(2)}, u32[]{:S(2)}) %collective-permute-start) | collective-permute-done | bytes 586784 | tf_op jit(solution)/shard_map/ppermute | solution.py:29
  149.2 3.4 multiply_convert_fusion.1
  154.1 4.7 collective-permute-start.1
  160.8 10.1 %collective-permute-done.1 = bf16[764,384]{1,0:T(8,128)(2,1)S(1)} collective-permute-done((bf16[764,384]{1,0:T(8,128)(2,1)S(1)}, bf16[764,384]{1,0:T(8,128)(2,1)S(1)}, u32[]{:S(2)}, u32[]{:S(2)}) %collective-permute-start.1) | collective-permute-done | bytes 586784 | tf_op jit(solution)/shard_map/ppermute | solution.py:29
  174.8 3.9 reshape.441
  186.4 4.0 reshape.468
  211.4 3.6 convert_reduce_fusion.2
  245.3 4.0 reshape.446
  255.6 4.0 reshape.444
  259.6 4.4 fusion.115
  273.1 7.4 %collective-permute-done.2 = bf16[764,384]{1,0:T(8,128)(2,1)S(1)} collective-permute-done((bf16[764,384]{1,0:T(8,128)(2,1)S(1)}, bf16[764,384]{1,0:T(8,128)(2,1)S(1)}, u32[]{:S(2)}, u32[]{:S(2)}) %collective-permute-start.2) | collective-permute-done | bytes 586784 | tf_op jit(solution)/shard_map/ppermute | solution.py:29
  284.2 4.3 convert_reduce_fusion.1
  316.5 4.5 fusion.124
  326.4 10.2 %collective-permute-done.3 = bf16[764,384]{1,0:T(8,128)(2,1)S(1)} collective-permute-done((bf16[764,384]{1,0:T(8,128)(2,1)S(1)}, bf16[764,384]{1,0:T(8,128)(2,1)S(1)}, u32[]{:S(2)}, u32[]{:S(2)}) %collective-permute-start.3) | collective-permute-done | bytes 586784 | tf_op jit(solution)/shard_map/ppermute | solution.py:29
  336.6 5.8 %convert_reduce_fusion = (f32[1536]{0:T(1024)}, bf16[764,1536]{1,0:T(8,128)(2,1)S(1)}) fusion(f32[764,1536]{1,0:T(8,128)} %get-tuple-element.117, f32[1536]{0:T(1024)S(1)} %copy-done.170, bf16[1920,384]{1,0:T(8,128)(2,1)S(1)} %copy-done.119, bf16[764,384]{1,0:T(8,128)(2,1)S(1)} %collective-permute-done.3, pred[]{:T(512)S(6)} %eq.5), kind=kOutput, calls=%fused_computation.21 | convolution fusion | flops 916798464 | bytes 8824833 | tf_op jit(solution)/shard_map/dot_general | solution.py:43
  353.1 3.9 fusion.225
  369.3 4.4 reshape.454
  402.7 3.5 fusion.80
  424.4 5.0 fusion.133
  433.8 59.0 %all-reduce.2 = f32[12,384]{1,0:T(8,128)S(1)} all-reduce(f32[12,384]{1,0:T(8,128)S(1)} %add_add_fusion), channel_id=4, replica_groups=mesh['section'=2,'dp'=16] {'dp'}, use_global_device_ids=true, to_apply=%region_68.69.clone | all-reduce | flops 4608 | bytes 36864
  (658 shorter events, 263.4 us)
Async XLA Ops:
  7.2 27.7 %copy-start.41 = (bf16[1528,384]{1,0:T(8,128)(2,1)S(1)}, bf16[1528,384]{1,0:T(8,128)(2,1)}, u32[]{:S(2)}) copy-start(bf16[1528,384]{1,0:T(8,128)(2,1)} %param.11) | copy-start | bytes 3520516
  7.2 47.6 %all-gather.4.cloned.1.call-start = ((), (), s32[]{:S(2)}) async-start(), calls=%async_computation.2 | async-start | bytes 2193408 | tf_op jit(solution)/shard_map/all_gather | solution.py:248
  9.0 86.7 %all-gather.6.cloned.1.call-start = ((), (), s32[]{:S(2)}) async-start(), calls=%async_computation.3 | async-start | bytes 1566720 | tf_op jit(solution)/shard_map/all_gather | solution.py:249
  10.6 489.5 %reduce-scatter.10.cloned.1.call-start = ((), (), s32[]{:S(2)}) async-start(), calls=%async_computation.5 | async-start | bytes 3133440
  34.8 60.9 %copy-start.181 = (f32[384]{0:T(512)}, f32[384]{0:T(512)S(1)}, u32[]{:S(2)}) copy-start(f32[384]{0:T(512)S(1)} %get-tuple-element.60) | copy-start | bytes 4612
  34.8 66.6 %copy-start.175 = (f32[384]{0:T(512)}, f32[384]{0:T(512)S(1)}, u32[]{:S(2)}) copy-start(f32[384]{0:T(512)S(1)} %get-tuple-element.57) | copy-start | bytes 4612
  34.8 85.1 %copy-start.151 = (f32[384]{0:T(512)}, f32[384]{0:T(512)S(1)}, u32[]{:S(2)}) copy-start(f32[384]{0:T(512)S(1)} %get-tuple-element.64) | copy-start | bytes 4612
  34.8 85.1 %copy-start.177 = (f32[384]{0:T(512)}, f32[384]{0:T(512)S(1)}, u32[]{:S(2)}) copy-start(f32[384]{0:T(512)S(1)} %get-tuple-element.63) | copy-start | bytes 4612
  35.1 22.2 %copy-start.145 = (f32[764]{0:T(1024)}, f32[764]{0:T(1024)S(1)}, u32[]{:S(2)}) copy-start(f32[764]{0:T(1024)S(1)} %broadcast_multiply_fusion.17) | copy-start | bytes 9172
  35.4 21.8 %copy-start.157 = (f32[764]{0:T(1024)}, f32[764]{0:T(1024)S(1)}, u32[]{:S(2)}) copy-start(f32[764]{0:T(1024)S(1)} %add_rsqrt_fusion.5) | copy-start | bytes 9172
  35.5 62.5 %copy-start.166 = (f32[1536]{0:T(1024)}, f32[1536]{0:T(1024)S(1)}, u32[]{:S(2)}) copy-start(f32[1536]{0:T(1024)S(1)} %add.366) | copy-start | bytes 18436
  35.5 84.5 %copy-start.171 = (f32[1152]{0:T(1024)}, f32[1152]{0:T(1024)S(1)}, u32[]{:S(2)}) copy-start(f32[1152]{0:T(1024)S(1)} %pad_maximum_fusion.24) | copy-start | bytes 13828
  74.0 21.7 %copy-start.42 = (bf16[1528,384]{1,0:T(8,128)(2,1)S(1)}, bf16[1528,384]{1,0:T(8,128)(2,1)}, u32[]{:S(2)}) copy-start(bf16[1528,384]{1,0:T(8,128)(2,1)} %param.11) | copy-start | bytes 3520516
  74.7 22.9 %copy-start.89 = (bf16[394,384]{0,1:T(8,128)(2,1)}, bf16[394,384]{0,1:T(8,128)(2,1)S(1)}, u32[]{:S(2)}) copy-start(bf16[394,384]{0,1:T(8,128)(2,1)S(1)} %reshape.432) | copy-start | bytes 907780
  102.8 16.4 %collective-permute-start = (bf16[764,384]{1,0:T(8,128)(2,1)S(1)}, bf16[764,384]{1,0:T(8,128)(2,1)S(1)}, u32[]{:S(2)}, u32[]{:S(2)}) collective-permute-start(bf16[764,384]{1,0:T(8,128)(2,1)S(1)} %fusion.59), channel_id=1, source_target_pairs={{0,16},{1,17},{2,18},{3,19},{4,20},{5,21},{6,22},{7,23},{8,24},{9,... | collective-permute-start | bytes 1760264 | tf_op jit(solution)/shard_map/ppermute | solution.py:29
  119.5 27.2 %copy-start.26 = (bf16[764,384]{1,0:T(8,128)(2,1)}, bf16[764,384]{1,0:T(8,128)(2,1)S(1)}, u32[]{:S(2)}) copy-start(bf16[764,384]{1,0:T(8,128)(2,1)S(1)} %get-tuple-element.74) | copy-start | bytes 1760260
  148.8 142.0 %copy-start.131 = (f32[764]{0:T(1024)}, f32[764]{0:T(1024)S(1)}, u32[]{:S(2)}) copy-start(f32[764]{0:T(1024)S(1)} %broadcast_multiply_fusion.14) | copy-start | bytes 9172
  154.1 16.7 %collective-permute-start.1 = (bf16[764,384]{1,0:T(8,128)(2,1)S(1)}, bf16[764,384]{1,0:T(8,128)(2,1)S(1)}, u32[]{:S(2)}, u32[]{:S(2)}) collective-permute-start(bf16[764,384]{1,0:T(8,128)(2,1)S(1)} %fusion.60), channel_id=1, source_target_pairs={{0,16},{1,17},{2,18},{3,19},{4,20},{5,21},{6,22},{7,23},{8,24},{9,... | collective-permute-start | bytes 1760264 | tf_op jit(solution)/shard_map/ppermute | solution.py:29
  264.6 15.9 %collective-permute-start.2 = (bf16[764,384]{1,0:T(8,128)(2,1)S(1)}, bf16[764,384]{1,0:T(8,128)(2,1)S(1)}, u32[]{:S(2)}, u32[]{:S(2)}) collective-permute-start(bf16[764,384]{1,0:T(8,128)(2,1)S(1)} %fusion.114), channel_id=1, source_target_pairs={{16,0},{17,1},{18,2},{19,3},{20,4},{21,5},{22,6},{23,7},{24,8},{25... | collective-permute-start | bytes 1760264 | tf_op jit(solution)/shard_map/ppermute | solution.py:29
  316.4 36.5 %copy-start.46 = (bf16[394,1152]{0,1:T(8,128)(2,1)}, bf16[394,1152]{0,1:T(8,128)(2,1)S(1)}, u32[]{:S(2)}) copy-start(bf16[394,1152]{0,1:T(8,128)(2,1)S(1)} %reshape.448) | copy-start | bytes 2723332
  321.5 15.1 %collective-permute-start.3 = (bf16[764,384]{1,0:T(8,128)(2,1)S(1)}, bf16[764,384]{1,0:T(8,128)(2,1)S(1)}, u32[]{:S(2)}, u32[]{:S(2)}) collective-permute-start(bf16[764,384]{1,0:T(8,128)(2,1)S(1)} %fusion.123), channel_id=1, source_target_pairs={{16,0},{17,1},{18,2},{19,3},{20,4},{21,5},{22,6},{23,7},{24,8},{25... | collective-permute-start | bytes 1760264 | tf_op jit(solution)/shard_map/ppermute | solution.py:29
  352.5 149.6 %reduce-scatter.8.cloned.1.call-start = ((), (), s32[]{:S(2)}) async-start(), calls=%async_computation.4 | async-start | bytes 4386816
  429.4 63.4 %copy-start.156 = (f32[1,12,24]{2,0,1:T(1,128)S(1)}, f32[1,12,24]{2,0,1:T(1,128)}, u32[]{:S(2)}) copy-start(f32[1,12,24]{2,0,1:T(1,128)} %param.19) | copy-start | bytes 3460
  429.4 67.4 %copy-start.11 = (f32[764,384]{1,0:T(8,128)S(1)}, f32[764,384]{1,0:T(8,128)}, u32[]{:S(2)}) copy-start(f32[764,384]{1,0:T(8,128)} %copy-done.10) | copy-start | bytes 3520516
  (181 other events, 671.1 us)
Sparse Core Ops, SparseCore 0:
  10.8 44.0 all-gather.3
  57.6 38.0 all-gather.5
  352.6 63.1 reduce-scatter.9
  419.5 71.7 reduce-scatter.7
where the time goes:
time: 517 us; the launch traced here: 511 us
  local copies, waits for them, and re-layouts  148 us (29%)
  matrix products  127 us (25%)
  blocking collectives  82.2 us (16%)
  waiting for transfers between devices  80.6 us (16%)
  other arithmetic  43.3 us (8%)
  between operations  17.3 us (3%)
  starting transfers between devices  12.1 us (2%)
    unnamed x1, blocking collectives  59 us
    ppermute x4, waiting for transfers between devices, from_behind(): lax.ppermute(value, axis, [(source, source + steps) for source in range(i...  40.2 us
    dot_general x12, matrix products, outer(): lax.dot_general(former, latter, (((1,), (1,)), ((), ())), preferred_eleme...  36.5 us
    unnamed x408, local copies, waits for them, and re-layouts  34.3 us
    dot_general x12, matrix products, product(): return jnp.dot(former, latter, preferred_element_type=jnp.float32)  28.1 us
    dot_general x12, matrix products, inner(): lax.dot_general(former, latter, (((0,), (0,)), ((), ())), preferred_eleme...  26.1 us
    all_gather x1, blocking collectives, per_device(): lax.all_gather(vectors[0].astype(jnp.bfloat16), 'dp', axis=1, tiled=True)  23.3 us
    reshape x9, local copies, waits for them, and re-layouts, attention_back(): return stacked.reshape(crop_count * length, 3 * HEADS * HEAD_DIM)  21.7 us
  transfers between devices with their start and end apart: 8, of which 6 were waited for; matrix products, arithmetic and copies ran while one was open for 23% of the time, Pallas kernels for 0%

commit v1 on v0

v1 whole, which is shorter than its diff:
```python
import functools

import jax
import jax.numpy as jnp
from jax import lax
from jax.experimental import pallas as pl
from jax.experimental.pallas import tpu as pltpu
from jax.sharding import PartitionSpec as P

D = 384
HEADS = 6
HEAD_DIM = 64
FF = 1536
GLOBAL = 2
GLOBAL_LEN = 197
LOCAL = 10
LOCAL_LEN = 37
STEP = 5
IMG_TOK = GLOBAL * GLOBAL_LEN + LOCAL * LOCAL_LEN

NORM_EPS = 1e-06
BETA_ONE = 0.5
BETA_TWO = 0.5
ADAM_EPS = 1e-08
RATE_MATRIX = 0.05
RATE_VECTOR = 0.2
DECAY = 0.05

ROWS = 768
BLOCK = 256
BLOCKS = ROWS // BLOCK
WINDOW = 208
WINDOWS = 4
CHUNK = 512
CHUNKS = FF // CHUNK
F32 = jnp.float32
BF16 = jnp.bfloat16


def window_start(index):
    return pl.multiple_of(jnp.minimum(index * 192, ROWS - WINDOW), 16)


def row_segment(row):
    local = ((row - GLOBAL * GLOBAL_LEN) * 1772) >> 16
    segment = jnp.where(row < GLOBAL * GLOBAL_LEN, jnp.where(row < GLOBAL_LEN, 0, 1), local + GLOBAL)
    return jnp.where(row < IMG_TOK, segment, 99)


def window_of(segment):
    return jnp.where(segment < 2, segment, jnp.where(segment < 7, 2, jnp.where(segment < 12, 3, 9)))


def dot(a, b):
    return jnp.dot(a, b, preferred_element_type=F32)


def dot_t(a, b):
    return lax.dot_general(a, b, (((1,), (1,)), ((), ())), preferred_element_type=F32)


def t_dot(a, b):
    return lax.dot_general(a, b, (((0,), (0,)), ((), ())), preferred_element_type=F32)


def standard(values):
    centre = values - jnp.mean(values, axis=-1, keepdims=True)
    inverse = lax.rsqrt(jnp.mean(centre * centre, axis=-1, keepdims=True) + NORM_EPS)
    return centre * inverse, inverse


def norm_back(normed, inverse, gain, incoming):
    scaled = incoming * gain
    return inverse * (
        scaled
        - jnp.mean(scaled, axis=-1, keepdims=True)
        - normed * jnp.mean(scaled * normed, axis=-1, keepdims=True)
    )


def gelu_pair(f):
    t = 1.0 / (1.0 + (0.3275911 * 0.7071067811865476) * jnp.abs(f))
    e = jnp.exp(-0.5 * f * f)
    poly = t * (
        0.5 * 0.254829592
        + t * (0.5 * -0.284496736 + t * (0.5 * 1.421413741 + t * (0.5 * -1.453152027 + t * (0.5 * 1.061405429))))
    )
    tail = poly * e
    below = jnp.where(f >= 0, 1.0 - tail, tail)
    return f * below, below + f * e * 0.3989422804014327


def column_sum(values):
    return jnp.sum(values, axis=0, keepdims=True)


def forward_layer(l, u_ref, out_ref, wide, tall, vec, s):
    def first(i, _):
        rows = pl.ds(pl.multiple_of(i * BLOCK, BLOCK), BLOCK)
        normed, _unused = standard(u_ref[rows, :].astype(F32))
        a = (normed * vec[l, 0:1, :] + vec[l, 1:2, :]).astype(BF16)
        s.a[l, rows, :] = a
        for third in range(3):
            cols = slice(third * D, (third + 1) * D)
            part = dot(a, wide[l, :, cols])
            if third != 1:
                part = part + vec[l, 2 + third // 2 : 3 + third // 2, :]
            s.qkv[l, rows, cols] = part.astype(BF16)
        return 0

    lax.fori_loop(0, BLOCKS, first, 0)
    s.o[l] = jnp.zeros((ROWS, D), BF16)
    low = lax.broadcasted_iota(jnp.int32, (1, 128), 1) < HEAD_DIM

    def attend(w, _):
        rows = pl.ds(window_start(w), WINDOW)
        bias = s.bias[w]
        for pair in range(HEADS // 2):
            base = pair * 128
            q = s.qkv[l, rows, base : base + 128]
            k = s.qkv[l, rows, D + base : D + base + 128]
            v = s.qkv[l, rows, 2 * D + base : 2 * D + base + 128]
            total = None
            for half in range(2):
                keep = low if half == 0 else jnp.logical_not(low)
                scores = dot_t(jnp.where(keep, k, jnp.zeros_like(k)), q) * (HEAD_DIM**-0.5) + bias
                top = jnp.maximum(jnp.max(scores, axis=0, keepdims=True), -1e20)
                weights = jnp.exp(scores - top)
                summed = jnp.sum(weights, axis=0, keepdims=True)
                weights = (weights * (1.0 / jnp.maximum(summed, 1e-20))).astype(BF16)
                s.p[l, w, 2 * pair + half] = weights
                part = t_dot(weights, jnp.where(keep, v, jnp.zeros_like(v)))
                total = part if total is None else total + part
            old = s.o[l, rows, base : base + 128]
            s.o[l, rows, base : base + 128] = old + total.astype(BF16)
        return 0

    lax.fori_loop(0, WINDOWS, attend, 0)

    def second(i, _):
        rows = pl.ds(pl.multiple_of(i * BLOCK, BLOCK), BLOCK)
        hidden = u_ref[rows, :].astype(F32) + dot(s.o[l, rows, :], tall[l, 0:D, :]) + vec[l, 4:5, :]
        s.h[l, rows, :] = hidden
        normed, _unused = standard(hidden)
        c = (normed * vec[l, 5:6, :] + vec[l, 6:7, :]).astype(BF16)
        s.c[l, rows, :] = c
        total = hidden + vec[l, 7:8, :]
        for j in range(CHUNKS):
            cols = slice(j * CHUNK, (j + 1) * CHUNK)
            f = dot(c, wide[l, :, 3 * D + j * CHUNK : 3 * D + (j + 1) * CHUNK]) + s.bup[l, 0:1, cols]
            value, slope = gelu_pair(f)
            z = value.astype(BF16)
            s.z[l, rows, cols] = z
            s.slope[l, rows, cols] = slope.astype(BF16)
            total = total + dot(z, tall[l, D + j * CHUNK : D + (j + 1) * CHUNK, :])
        out_ref[rows, :] = total.astype(BF16)
        return 0

    lax.fori_loop(0, BLOCKS, second, 0)


def backward_layer(l, u_ref, dy_ref, du_ref, wide, tall, vec, gwide, gtall, gvec, s):
    gvec[l] = jnp.zeros_like(gvec[l])
    s.dbup[...] = jnp.zeros_like(s.dbup)

    def first(i, _):
        rows = pl.ds(pl.multiple_of(i * BLOCK, BLOCK), BLOCK)
        dy = dy_ref[rows, :]
        dc = jnp.zeros((BLOCK, D), F32)
        for j in range(CHUNKS):
            cols = slice(j * CHUNK, (j + 1) * CHUNK)
            dz = dot_t(dy, tall[l, D + j * CHUNK : D + (j + 1) * CHUNK, :])
            df = (dz * s.slope[l, rows, cols].astype(F32)).astype(BF16)
            s.df[rows, cols] = df
            s.dbup[0:1, cols] += column_sum(df.astype(F32))
            dc = dc + dot_t(df, wide[l, :, 3 * D + j * CHUNK : 3 * D + (j + 1) * CHUNK])
        normed, inverse = standard(s.h[l, rows, :])
        top = dy.astype(F32)
        dh = top + norm_back(normed, inverse, vec[l, 5:6, :], dc)
        s.dh[rows, :] = dh
        dhb = dh.astype(BF16)
        s.dhb[rows, :] = dhb
        s.dout[rows, :] = dot_t(dhb, tall[l, 0:D, :]).astype(BF16)
        gvec[l, 4:5, :] += column_sum(dhb.astype(F32))
        gvec[l, 5:6, :] += column_sum(dc * normed)
        gvec[l, 6:7, :] += column_sum(dc)
        gvec[l, 7:8, :] += column_sum(top)
        return 0

    lax.fori_loop(0, BLOCKS, first, 0)
    for j in range(FF // D):
        gvec[l, 8 + j : 9 + j, :] = s.dbup[0:1, j * D : (j + 1) * D]

    def down(i, _):
        cols = pl.ds(pl.multiple_of(i * BLOCK, BLOCK), BLOCK)
        gtall[l, pl.ds(pl.multiple_of(D + i * BLOCK, 128), BLOCK), :] = t_dot(s.z[l, :, cols], dy_ref[...]).astype(gtall.dtype)
        return 0

    lax.fori_loop(0, FF // BLOCK, down, 0)

    def up(i, _):
        cols = pl.ds(pl.multiple_of(i * BLOCK, BLOCK), BLOCK)
        gwide[l, :, pl.ds(pl.multiple_of(3 * D + i * BLOCK, 128), BLOCK)] = t_dot(s.c[l], s.df[:, cols]).astype(gwide.dtype)
        return 0

    lax.fori_loop(0, FF // BLOCK, up, 0)
    gtall[l, 0:D, :] = t_dot(s.o[l], s.dhb[...]).astype(gtall.dtype)

    s.dqkv[...] = jnp.zeros_like(s.dqkv)
    low = lax.broadcasted_iota(jnp.int32, (1, 128), 1) < HEAD_DIM

    def attend(w, _):
        rows = pl.ds(window_start(w), WINDOW)
        for pair in range(HEADS // 2):
            base = pair * 128
            q = s.qkv[l, rows, base : base + 128]
            k = s.qkv[l, rows, D + base : D + base + 128]
            v = s.qkv[l, rows, 2 * D + base : 2 * D + base + 128]
            grad = s.dout[rows, base : base + 128]
            dq = dk = dv = None
            for half in range(2):
                keep = low if half == 0 else jnp.logical_not(low)

                def only(x, keep=keep):
                    return jnp.where(keep, x, jnp.zeros_like(x))

                weights = s.p[l, w, 2 * pair + half]
                grad_half = only(grad)
                dv_part = dot(weights, grad_half)
                dp = dot_t(v, grad_half)
                wide_weights = weights.astype(F32)
                product = dp * wide_weights
                ds = (product - wide_weights * jnp.sum(product, axis=0, keepdims=True)).astype(BF16)
                dk_part = dot(ds, only(q))
                dq_part = t_dot(ds, only(k))
                if half == 0:
                    dq, dk, dv = dq_part, dk_part, dv_part
                else:
                    dq, dk, dv = dq + dq_part, dk + dk_part, dv + dv_part
            scale = HEAD_DIM**-0.5
            for offset, value in ((0, dq * scale), (D, dk * scale), (2 * D, dv)):
                cols = slice(offset + base, offset + base + 128)
                s.dqkv[rows, cols] = s.dqkv[rows, cols] + value.astype(BF16)
        return 0

    lax.fori_loop(0, WINDOWS, attend, 0)

    def last(i, _):
        rows = pl.ds(pl.multiple_of(i * BLOCK, BLOCK), BLOCK)
        dqkv = s.dqkv[rows, :]
        da = dot_t(dqkv, wide[l, :, 0 : 3 * D])
        normed, inverse = standard(u_ref[rows, :].astype(F32))
        du = s.dh[rows, :] + norm_back(normed, inverse, vec[l, 0:1, :], da)
        du_ref[rows, :] = du.astype(BF16)
        gvec[l, 0:1, :] += column_sum(da * normed)
        gvec[l, 1:2, :] += column_sum(da)
        gvec[l, 2:3, :] += column_sum(dqkv[:, 0:D].astype(F32))
        gvec[l, 3:4, :] += column_sum(dqkv[:, 2 * D : 3 * D].astype(F32))
        return 0

    lax.fori_loop(0, BLOCKS, last, 0)

    def mix(i, _):
        cols = pl.ds(pl.multiple_of(i * D, 128), D)
        gwide[l, :, cols] = t_dot(s.a[l], s.dqkv[:, cols]).astype(gwide.dtype)
        return 0

    lax.fori_loop(0, 3, mix, 0)


class Scratch:
    pass


SCRATCH = (
    ("a", (2, ROWS, D), BF16),
    ("qkv", (2, ROWS, 3 * D), BF16),
    ("o", (2, ROWS, D), BF16),
    ("h", (2, ROWS, D), F32),
    ("c", (2, ROWS, D), BF16),
    ("z", (2, ROWS, FF), BF16),
    ("slope", (2, ROWS, FF), BF16),
    ("p", (2, WINDOWS, HEADS, WINDOW, WINDOW), BF16),
    ("bias", (WINDOWS, WINDOW, WINDOW), F32),
    ("bup", (2, 8, FF), F32),
    ("dbup", (8, FF), F32),
    ("df", (ROWS, FF), BF16),
    ("dh", (ROWS, D), F32),
    ("dhb", (ROWS, D), BF16),
    ("dout", (ROWS, D), BF16),
    ("dqkv", (ROWS, 3 * D), BF16),
)


def image_kernel(x, cot, wide, tall, vec, act, grads, gwide, gtall, gvec, *scratch):
    s = Scratch()
    for (name, _, _), ref in zip(SCRATCH, scratch):
        setattr(s, name, ref)

    def fill(w, _):
        start = window_start(w)
        key = row_segment(start + lax.broadcasted_iota(jnp.int32, (WINDOW, 1), 0))
        query = row_segment(start + lax.broadcasted_iota(jnp.int32, (1, WINDOW), 1))
        inside = (key == query) & (window_of(key) == w)
        s.bias[w] = jnp.where(inside, 0.0, -1e30).astype(F32)
        return 0

    lax.fori_loop(0, WINDOWS, fill, 0)
    for l in range(2):
        for j in range(FF // D):
            s.bup[l, 0:1, j * D : (j + 1) * D] = vec[l, 8 + j : 9 + j, :]
    forward_layer(0, x, act.at[0], wide, tall, vec, s)
    forward_layer(1, act.at[0], act.at[1], wide, tall, vec, s)
    backward_layer(1, act.at[0], cot, grads.at[1], wide, tall, vec, gwide, gtall, gvec, s)
    backward_layer(0, x, grads.at[1], grads.at[0], wide, tall, vec, gwide, gtall, gvec, s)


def one_image(x, cot, wide, tall, vec):
    whole = pl.BlockSpec(memory_space=pltpu.VMEM)
    return pl.pallas_call(
        image_kernel,
        out_shape=(
            jax.ShapeDtypeStruct((2, ROWS, D), BF16),
            jax.ShapeDtypeStruct((2, ROWS, D), BF16),
            jax.ShapeDtypeStruct(wide.shape, BF16),
            jax.ShapeDtypeStruct(tall.shape, BF16),
            jax.ShapeDtypeStruct(vec.shape, F32),
        ),
        in_specs=[whole] * 5,
        out_specs=(whole,) * 5,
        scratch_shapes=[pltpu.VMEM(shape, dtype) for _, shape, dtype in SCRATCH],
        compiler_params=pltpu.CompilerParams(vmem_limit_bytes=63 * 2**20),
        cost_estimate=pl.CostEstimate(flops=18 * 10**9, bytes_accessed=20 * 10**6, transcendentals=10**7),
    )(x, cot, wide, tall, vec)


def adamw(weights, first, second, grads, rate, decay):
    first_new = BETA_ONE * first + (1.0 - BETA_ONE) * grads
    second_new = BETA_TWO * second + (1.0 - BETA_TWO) * grads * grads
    corrected = (
        first_new
        / (1.0 - BETA_ONE**STEP)
        / (jnp.sqrt(second_new / (1.0 - BETA_TWO**STEP)) + ADAM_EPS)
    )
    return (first_new, second_new, weights - rate * (corrected + decay * weights))


def per_device(
    inputs, cotangent, wide_weights, wide_first, wide_second, tall_weights, tall_first, tall_second,
    vectors, vector_first, vector_second,
):
    section = lax.axis_index("section")
    both = ("section", "dp")
    wide = lax.all_gather(wide_weights[0].astype(BF16), both, axis=0, tiled=True).reshape(2, -1, 3 * D + FF)
    tall = lax.all_gather(tall_weights[0].astype(BF16), both, axis=0, tiled=True).reshape(2, -1, D)
    vec = lax.all_gather(vectors[0].astype(BF16), "dp", axis=1, tiled=True)
    vec = lax.all_gather(vec, "section", axis=0, tiled=False).astype(F32)
    vec = jnp.pad(vec, ((0, 0), (0, 4), (0, 0)))

    def own(array):
        return jnp.pad(lax.dynamic_slice_in_dim(array, section * IMG_TOK, IMG_TOK), ((0, ROWS - IMG_TOK), (0, 0)))

    act, grads, gwide, gtall, gvec = one_image(own(inputs), own(cotangent), wide, tall, vec)

    def exchange(array):
        array = array[:, :IMG_TOK]
        mine = lax.dynamic_index_in_dim(array, section, keepdims=False)
        other = lax.dynamic_index_in_dim(array, 1 - section, keepdims=False)
        other = lax.ppermute(other, "section", [(0, 1), (1, 0)])
        return jnp.where(section == 0, jnp.concatenate((mine, other)), jnp.concatenate((other, mine)))

    def reduced(array):
        array = lax.psum_scatter(array, "section", scatter_dimension=0, tiled=False)
        return lax.psum_scatter(array, "dp", scatter_dimension=0, tiled=True).astype(F32)

    total_wide = reduced(gwide)
    total_tall = reduced(gtall)
    total_vec = lax.psum_scatter(gvec[:, :12], "section", scatter_dimension=0, tiled=False)
    total_vec = lax.psum_scatter(total_vec, "dp", scatter_dimension=1, tiled=True)
    wide_m, wide_s, wide_n = adamw(wide_weights[0], wide_first[0], wide_second[0], total_wide, RATE_MATRIX, DECAY)
    tall_m, tall_s, tall_n = adamw(tall_weights[0], tall_first[0], tall_second[0], total_tall, RATE_MATRIX, DECAY)
    vec_m, vec_s, vec_n = adamw(vectors[0], vector_first[0], vector_second[0], total_vec, RATE_VECTOR, 0.0)
    outs = (exchange(act), exchange(grads), wide_m, wide_s, wide_n, tall_m, tall_s, tall_n, vec_m, vec_s, vec_n)
    return tuple(out[None] for out in outs)


def solution(mesh):
    data = P("dp", None)
    matrix = P("section", "dp", None)
    vector = P("section", None, "dp")
    in_specs = (data, data) + (matrix,) * 6 + (vector,) * 3
    out_specs = (matrix,) * 8 + (vector,) * 3
    return jax.shard_map(per_device, mesh=mesh, in_specs=in_specs, out_specs=out_specs, check_vma=False)
```

time: 517 us -> 456 us (0.88); the launches traced: 511 us -> 455 us
  waiting for transfers between devices: 80.6 us -> 257 us
  local copies, waits for them, and re-layouts: 148 us -> 7.51 us
  matrix products: 127 us -> 0 us
  Pallas kernels: 0 us -> 73.6 us
  other arithmetic: 43.3 us -> 11.2 us
  starting transfers between devices: 12.1 us -> 1.68 us
  blocking collectives: 82.2 us -> 89.5 us
    dot_general x72 -> x0, matrix products: 127 us -> none  [the longest x12 36.5 us: outer(): lax.dot_general(former, latter, (((1,), (1,)), ((), ())), preferred_eleme...]
    reduce_scatter x0 -> x3, waiting for transfers between devices: none -> 103 us  [the longest x2 94.7 us: reduced(): array = lax.psum_scatter(array, 'section', scatter_dimension=0, tiled=False)]
    pallas_call x0 -> x1, Pallas kernels: none -> 73.6 us  [one_image(): pl.pallas_call(image_kernel, out_shape=(jax.ShapeDtypeStruct((2, ROWS, D)...]
    reshape x36 -> x0, local copies, waits for them, and re-layouts: 62.1 us -> none  [the longest x9 21.7 us: attention_back(): return stacked.reshape(crop_count * length, 3 * HEADS * HEAD_DIM)]
    unnamed x6 -> x9, waiting for transfers between devices: 0.07 us -> 59.4 us
    all_gather x2, waiting for transfers between devices: 40.3 us -> 94.6 us  [the longest x1 63.9 us: per_device(): lax.all_gather(wide_weights[0].astype(BF16), both, axis=0, tiled=True)]
    ppermute x4 -> x2, waiting for transfers between devices: 40.2 us -> 0.01 us  [exchange(): other = lax.ppermute(other, 'section', [(0, 1), (1, 0)])]
    unnamed x408 -> x26, local copies, waits for them, and re-layouts: 34.3 us -> 3.96 us
  transfers between devices with their start and end apart: 8 -> 9, of which waited for: 6 -> 6; matrix products, arithmetic and copies ran while one was open for 23% -> 3% of each run, Pallas kernels for 0% -> 0%
where the time goes in v1:
time: 456 us; the launch traced here: 455 us
  waiting for transfers between devices  257 us (56%)
  blocking collectives  89.5 us (20%)
  Pallas kernels  73.6 us (16%)
  between operations  14.9 us (3%)
  other arithmetic  11.2 us (2%)
  local copies, waits for them, and re-layouts  7.51 us (2%)
    reduce_scatter x2, waiting for transfers between devices, reduced(): array = lax.psum_scatter(array, 'section', scatter_dimension=0, tiled=False)  94.7 us
    pallas_call x1, Pallas kernels, one_image(): pl.pallas_call(image_kernel, out_shape=(jax.ShapeDtypeStruct((2, ROWS, D)...  73.6 us
    all_gather x1, waiting for transfers between devices, per_device(): lax.all_gather(wide_weights[0].astype(BF16), both, axis=0, tiled=True)  63.9 us
    unnamed x1, blocking collectives  61.9 us
    unnamed x9, waiting for transfers between devices  59.4 us
    all_gather x1, waiting for transfers between devices, per_device(): lax.all_gather(tall_weights[0].astype(BF16), both, axis=0, tiled=True)  30.7 us
    all_gather x1, blocking collectives, per_device(): vec = lax.all_gather(vectors[0].astype(BF16), 'dp', axis=1, tiled=True)  23.2 us
  transfers between devices with their start and end apart: 9, of which 6 were waited for; matrix products, arithmetic and copies ran while one was open for 3% of the time, Pallas kernels for 0%

profile of v1, /device:TPU:0, one launch (start us, length us, event | category | flops | bytes accessed | tf_op | source)
XLA Modules:
  0.0 455.4 jit_solution(7089354320086719245)
XLA Ops:
  7.2 1.6 bitcast_convert_fusion.1
  8.9 1.6 bitcast_convert_fusion
  10.6 1.5 constant_dynamic-slice_fusion.2
  12.1 0.9 pad.13.x
  13.0 0.9 pad.14.cot
  13.9 23.2 %all-gather.1 = bf16[16,24,12]{1,2,0:T(8,128)(2,1)S(1)} all-gather(bf16[1,24,12]{1,2,0:T(8,128)(2,1)S(1)} %bitcast.129), channel_id=1, replica_groups=mesh['section'=2,'dp'=16] {'dp'}, dimensions={0}, use_global_device_ids=true | all-gather | bytes 9792 | tf_op jit(solution)/shard_map/all_gather | solution.py:356
  37.3 4.4 all-gather.2
  41.7 0.6 pad_convert_fusion.vec
  42.3 30.7 %all-gather.8.cloned.1.call-done = bf16[3840,384]{1,0:T(8,128)(2,1)} async-done(((bf16[120,384]{1,0:T(8,128)(2,1)}), bf16[3840,384]{1,0:T(8,128)(2,1)}) %all-gather.8.cloned.1.call-update) | async-done | bytes 2949136 | tf_op jit(solution)/shard_map/all_gather | solution.py:355
  73.0 63.9 %all-gather.6.cloned.1.call-done = bf16[768,2688]{1,0:T(8,128)(2,1)} async-done(((bf16[24,2688]{1,0:T(8,128)(2,1)}), bf16[768,2688]{1,0:T(8,128)(2,1)}) %all-gather.6.cloned.1.call-update) | async-done | bytes 4128784 | tf_op jit(solution)/shard_map/all_gather | solution.py:354
  136.9 73.6 %shard_map.194 = (bf16[2,768,384]{2,1,0:T(8,128)(2,1)}, bf16[2,768,384]{2,1,0:T(8,128)(2,1)}, bf16[2,384,2688]{2,1,0:T(8,128)(2,1)}, bf16[2,1920,384]{2,1,0:T(8,128)(2,1)}, f32[2,16,384]{2,1,0:T(8,128)}) custom-call(bf16[768,384]{1,0:T(8,128)(2,1)} %pad.13.x, bf16[768,384]{1,0:T(8,128)(2,1)} %pad.14.cot, bf16[2,384,2688]{2,1,0:T(8,128)(2,1)} %bitcast.130, ...), custom_call_target="tpu_custom_call" | custom-call | flops 17999998976 | bytes 20000000 | tf_op jit(solution)/shard_map/pallas_call | solution.py:320
  211.7 38.8 %reduce-scatter.13.cloned.1.call-done = bf16[1,1920,384]{2,1,0:T(8,128)(2,1)} async-done(((bf16[2,1920,384]{2,1,0:T(8,128)(2,1)}), bf16[1,1920,384]{2,1,0:T(8,128)(2,1)}) %reduce-scatter.13.cloned.1.call-update) | async-done | bytes 1474576 | tf_op jit(solution)/shard_map/reduce_scatter | solution.py:373
  250.6 55.9 %reduce-scatter.11.cloned.1.call-done = bf16[1,384,2688]{2,1,0:T(8,128)(2,1)} async-done(((bf16[2,384,2688]{2,1,0:T(8,128)(2,1)}), bf16[1,384,2688]{2,1,0:T(8,128)(2,1)}) %reduce-scatter.11.cloned.1.call-update) | async-done | bytes 2064400 | tf_op jit(solution)/shard_map/reduce_scatter | solution.py:373
  307.0 0.8 copy-done
  307.9 1.0 collective-permute-start
  309.0 1.2 dynamic-slice
  310.8 8.3 %reduce-scatter.15.cloned.1.call-done = f32[1,12,384]{2,1,0:T(8,128)} async-done(((f32[2,12,384]{2,1,0:T(8,128)}), f32[1,12,384]{2,1,0:T(8,128)}) %reduce-scatter.15.cloned.1.call-update) | async-done | bytes 18448 | tf_op jit(solution)/shard_map/reduce_scatter | solution.py:378
  319.1 61.9 %all-reduce.5 = f32[12,384]{1,0:T(8,128)} all-reduce(f32[12,384]{1,0:T(8,128)} %bitcast.128), channel_id=8, replica_groups=mesh['section'=2,'dp'=16] {'dp'}, use_global_device_ids=true, to_apply=%region_5.6.clone | all-reduce | flops 4608 | bytes 36864
  381.0 0.8 fusion.15
  383.6 1.4 maximum_select_fusion.1
  385.1 1.4 maximum_select_fusion
  386.6 1.8 fusion.7
  388.4 58.3 %reduce-scatter.17.cloned.1.call-done = bf16[24,2688]{1,0:T(8,128)(2,1)} async-done(((bf16[384,2688]{1,0:T(8,128)(2,1)}), bf16[24,2688]{1,0:T(8,128)(2,1)}) %reduce-scatter.17.cloned.1.call-update) | async-done | bytes 129040
  446.7 1.9 fusion.3
  (45 shorter events, 4.0 us)
Async XLA Ops:
  7.2 65.8 %all-gather.8.cloned.1.call-start = ((), (), s32[]{:S(2)}) async-start(), calls=%async_computation.6 | async-start | bytes 3041280 | tf_op jit(solution)/shard_map/all_gather | solution.py:355
  8.8 128.1 %all-gather.6.cloned.1.call-start = ((), (), s32[]{:S(2)}) async-start(), calls=%async_computation.5 | async-start | bytes 4257792 | tf_op jit(solution)/shard_map/all_gather | solution.py:354
  10.5 240.0 %reduce-scatter.13.cloned.1.call-start = ((), (), s32[]{:S(2)}) async-start(), calls=%async_computation.8 | async-start | bytes 4423680 | tf_op jit(solution)/shard_map/reduce_scatter | solution.py:373
  12.1 1.8 copy-start.8
  210.5 96.0 %reduce-scatter.11.cloned.1.call-start = ((), (), s32[]{:S(2)}) async-start(), calls=%async_computation.7 | async-start | bytes 6193152 | tf_op jit(solution)/shard_map/reduce_scatter | solution.py:373
  211.1 108.0 %reduce-scatter.15.cloned.1.call-start = ((), (), s32[]{:S(2)}) async-start(), calls=%async_computation.9 | async-start | bytes 73728 | tf_op jit(solution)/shard_map/reduce_scatter | solution.py:378
  211.7 174.8 %reduce-scatter.19.cloned.1.call-start = ((), (), s32[]{:S(2)}) async-start(), calls=%async_computation.11 | async-start | bytes 1566720
  250.6 55.9 %copy-start.1 = (bf16[2,768,384]{2,1,0:T(8,128)(2,1)S(1)}, bf16[2,768,384]{2,1,0:T(8,128)(2,1)}, u32[]{:S(2)}) copy-start(bf16[2,768,384]{2,1,0:T(8,128)(2,1)} %get-tuple-element.17) | copy-start | bytes 3538948
  250.6 196.1 %reduce-scatter.17.cloned.1.call-start = ((), (), s32[]{:S(2)}) async-start(), calls=%async_computation.10 | async-start | bytes 2193408
  306.5 1.3 copy-start
  306.7 76.9 %collective-permute-start.1 = (bf16[764,384]{1,0:T(8,128)(2,1)S(1)}, bf16[764,384]{1,0:T(8,128)(2,1)S(1)}, u32[]{:S(2)}, u32[]{:S(2)}) collective-permute-start(bf16[764,384]{1,0:T(8,128)(2,1)S(1)} %get-tuple-element.55), channel_id=1, source_target_pairs={{0,16},{16,0},{1,17},{17,1},{2,18},{18,2},{3,19},{19,3},{4,20},{20... | collective-permute-start | bytes 1760264 | tf_op jit(solution)/shard_map/ppermute | solution.py:369
  307.8 73.2 %copy-start.9 = (f32[1,12,24]{2,0,1:T(1,128)S(1)}, f32[1,12,24]{2,0,1:T(1,128)}, u32[]{:S(2)}) copy-start(f32[1,12,24]{2,0,1:T(1,128)} %param.20) | copy-start | bytes 3460
  307.9 77.2 %collective-permute-start = (bf16[764,384]{1,0:T(8,128)(2,1)S(1)}, bf16[764,384]{1,0:T(8,128)(2,1)S(1)}, u32[]{:S(2)}, u32[]{:S(2)}) collective-permute-start(bf16[764,384]{1,0:T(8,128)(2,1)S(1)} %get-tuple-element.57), channel_id=1, source_target_pairs={{0,16},{16,0},{1,17},{17,1},{2,18},{18,2},{3,19},{19,3},{4,20},{20... | collective-permute-start | bytes 1760264 | tf_op jit(solution)/shard_map/ppermute | solution.py:369
  385.1 1.5 copy-start.3
  385.1 1.5 copy-start.6
  385.1 1.5 copy-start.7
  386.5 60.2 %copy-start.2 = (f32[1,24,2688]{2,1,0:T(8,128)S(1)}, f32[1,24,2688]{2,1,0:T(8,128)}, u32[]{:S(2)}) copy-start(f32[1,24,2688]{2,1,0:T(8,128)} %param.13) | copy-start | bytes 774148
  386.5 60.2 %copy-start.4 = (f32[1,24,2688]{2,1,0:T(8,128)S(1)}, f32[1,24,2688]{2,1,0:T(8,128)}, u32[]{:S(2)}) copy-start(f32[1,24,2688]{2,1,0:T(8,128)} %param.14) | copy-start | bytes 774148
  386.5 60.2 %copy-start.5 = (f32[1,24,2688]{2,1,0:T(8,128)S(1)}, f32[1,24,2688]{2,1,0:T(8,128)}, u32[]{:S(2)}) copy-start(f32[1,24,2688]{2,1,0:T(8,128)} %param.15) | copy-start | bytes 774148
Sparse Core Ops, SparseCore 0:
  11.4 61.5 all-gather.7
  76.4 60.4 all-gather.5
  210.7 39.8 reduce-scatter.12
  252.8 53.6 reduce-scatter.10
  309.2 9.9 reduce-scatter.14
  323.2 58.8 reduce-scatter.18
  386.3 60.2 reduce-scatter.16

commit v2 on v1

v2 whole, which is shorter than its diff:
```python
import functools

import jax
import jax.numpy as jnp
from jax import lax
from jax.experimental import pallas as pl
from jax.experimental.pallas import tpu as pltpu
from jax.sharding import PartitionSpec as P

D = 384
HEADS = 6
HEAD_DIM = 64
FF = 1536
GLOBAL = 2
GLOBAL_LEN = 197
LOCAL = 10
LOCAL_LEN = 37
STEP = 5
IMG_TOK = GLOBAL * GLOBAL_LEN + LOCAL * LOCAL_LEN

NORM_EPS = 1e-06
BETA_ONE = 0.5
BETA_TWO = 0.5
ADAM_EPS = 1e-08
RATE_MATRIX = 0.05
RATE_VECTOR = 0.2
DECAY = 0.05

ROWS = 768
BLOCK = 256
BLOCKS = ROWS // BLOCK
WINDOW = 208
WINDOWS = 4
CHUNK = 512
CHUNKS = FF // CHUNK
TILE = 16
SLOTS = 8
HALF = 19 * TILE
STAGES = ((0, 6 * TILE), (6 * TILE, 7 * TILE), (13 * TILE, 6 * TILE))
MESH = pl.DeviceIdType.MESH
F32 = jnp.float32
BF16 = jnp.bfloat16


def window_start(index):
    return pl.multiple_of(jnp.minimum(index * 192, ROWS - WINDOW), 16)


def row_segment(row):
    local = ((row - GLOBAL * GLOBAL_LEN) * 1772) >> 16
    segment = jnp.where(row < GLOBAL * GLOBAL_LEN, jnp.where(row < GLOBAL_LEN, 0, 1), local + GLOBAL)
    return jnp.where(row < IMG_TOK, segment, 99)


def window_of(segment):
    return jnp.where(segment < 2, segment, jnp.where(segment < 7, 2, jnp.where(segment < 12, 3, 9)))


def dot(a, b):
    return jnp.dot(a, b, preferred_element_type=F32)


def dot_t(a, b):
    return lax.dot_general(a, b, (((1,), (1,)), ((), ())), preferred_element_type=F32)


def t_dot(a, b):
    return lax.dot_general(a, b, (((0,), (0,)), ((), ())), preferred_element_type=F32)


def standard(values):
    centre = values - jnp.mean(values, axis=-1, keepdims=True)
    inverse = lax.rsqrt(jnp.mean(centre * centre, axis=-1, keepdims=True) + NORM_EPS)
    return centre * inverse, inverse


def norm_back(normed, inverse, gain, incoming):
    scaled = incoming * gain
    return inverse * (
        scaled
        - jnp.mean(scaled, axis=-1, keepdims=True)
        - normed * jnp.mean(scaled * normed, axis=-1, keepdims=True)
    )


def gelu_pair(f):
    t = 1.0 / (1.0 + (0.3275911 * 0.7071067811865476) * jnp.abs(f))
    e = jnp.exp(-0.5 * f * f)
    poly = t * (
        0.5 * 0.254829592
        + t * (0.5 * -0.284496736 + t * (0.5 * 1.421413741 + t * (0.5 * -1.453152027 + t * (0.5 * 1.061405429))))
    )
    tail = poly * e
    below = jnp.where(f >= 0, 1.0 - tail, tail)
    return f * below, below + f * e * 0.3989422804014327


def column_sum(values):
    return jnp.sum(values, axis=0, keepdims=True)


def qkv_tile(i):
    return i if i < 5 else 19 + i - 5


def tall_tile(i):
    return 6 + i if i < 7 else (23 if i == 7 else 25 + i - 8)


def up_tile(i):
    return 13 + i if i < 6 else 32 + i - 6


def vec_tile(half):
    return 19 * half + 5


def runs(tiles):
    out = []
    for slot, tile in tiles:
        if out and out[-1][0] == slot and out[-1][1] + out[-1][2] == tile * TILE:
            out[-1][2] += TILE
        else:
            out.append([slot, tile * TILE, TILE])
    return out


def wide_tiles(name, block):
    return [(k, name(3 * block + i)) for k in range(SLOTS) for i in range(3)]


def tall_tiles(first, count):
    per = 15
    return [(t // per, tall_tile(t % per)) for t in range(first // TILE, (first + count) // TILE)]


def load_rows(ref, l, tiles, lanes=slice(0, D)):
    return jnp.concatenate(
        [ref[l, slot // 2, slot % 2, row : row + count, lanes] for slot, row, count in runs(tiles)], axis=0
    )


def store_rows(ref, l, tiles, value):
    done = 0
    for slot, row, count in runs(tiles):
        ref[l, slot // 2, slot % 2, row : row + count, :] = value[done : done + count]
        done += count


def load_qkv(w, l):
    return jnp.concatenate([load_rows(w, l, wide_tiles(qkv_tile, b)) for b in range(3)], axis=1)


def load_up(w, l, j):
    parts, at = [], j * CHUNK
    while at < (j + 1) * CHUNK:
        block, lane = divmod(at, D)
        take = min(D - lane, (j + 1) * CHUNK - at)
        parts.append(load_rows(w, l, wide_tiles(up_tile, block), slice(lane, lane + take)))
        at += take
    return jnp.concatenate(parts, axis=1)


def load_proj(w, l):
    return load_rows(w, l, tall_tiles(0, D))


def load_down(w, l, j):
    return load_rows(w, l, tall_tiles(D + j * CHUNK, CHUNK))


def row_block(i):
    return pl.ds(pl.multiple_of(i * BLOCK, BLOCK), BLOCK)


class Image:
    def __init__(self, s):
        self.s = s
        self.low = None

    def gains(self, l):
        s = self.s
        lane = lax.broadcasted_iota(jnp.int32, (TILE, 128), 1)
        tiles = [jnp.zeros((TILE, 128), F32) for _ in range(D // 128)]
        for slot in range(SLOTS):
            for half in range(2):
                row = vec_tile(half) * TILE
                part = s.w[l, slot // 2, slot % 2, row : row + TILE, 0:128].astype(F32)
                width = D // (2 * SLOTS)
                at = (2 * slot + half) * width
                index, shift = divmod(at, 128)
                moved = pltpu.roll(part, shift, 1) if shift else part
                if shift + width > 128:
                    tiles[index] = tiles[index] + jnp.where(lane >= shift, moved, 0.0)
                    tiles[index + 1] = tiles[index + 1] + jnp.where(lane < shift, moved, 0.0)
                else:
                    tiles[index] = tiles[index] + moved
        for index, tile in enumerate(tiles):
            s.vec[l, :, index * 128 : (index + 1) * 128] = tile
        for j in range(FF // D):
            s.bup[l, 0:1, j * D : (j + 1) * D] = s.vec[l, 8 + j : 9 + j, :]

    def spread_gains(self, l):
        s = self.s
        lane = lax.broadcasted_iota(jnp.int32, (TILE, 128), 1)
        width = D // (2 * SLOTS)
        for slot in range(SLOTS):
            for half in range(2):
                at = (2 * slot + half) * width
                index, shift = divmod(at, 128)
                tile = s.gvec[l, :, index * 128 : (index + 1) * 128]
                if shift + width > 128:
                    tile = jnp.where(lane >= shift, tile, s.gvec[l, :, (index + 1) * 128 : (index + 2) * 128])
                moved = pltpu.roll(tile, 128 - shift, 1) if shift else tile
                moved = jnp.where(lane < width, moved, 0.0).astype(BF16)
                row = vec_tile(half) * TILE
                s.g[l, slot // 2, slot % 2, row : row + TILE, :] = jnp.concatenate(
                    (moved, jnp.zeros((TILE, D - 128), BF16)), axis=1
                )

    def fill_bias(self):
        s = self.s

        def fill(w, _):
            start = window_start(w)
            key = row_segment(start + lax.broadcasted_iota(jnp.int32, (WINDOW, 1), 0))
            query = row_segment(start + lax.broadcasted_iota(jnp.int32, (1, WINDOW), 1))
            inside = (key == query) & (window_of(key) == w)
            s.bias[w] = jnp.where(inside, 0.0, -1e30).astype(F32)
            return 0

        lax.fori_loop(0, WINDOWS, fill, 0)

    def forward_first(self, l, u_ref):
        s = self.s

        def step(i, _):
            rows = row_block(i)
            normed, _unused = standard(u_ref[rows, :].astype(F32))
            a = (normed * s.vec[l, 0:1, :] + s.vec[l, 1:2, :]).astype(BF16)
            s.a[l, rows, :] = a
            part = dot(a, load_qkv(s.w, l))
            s.qkv[l, rows, 0:D] = (part[:, 0:D] + s.vec[l, 2:3, :]).astype(BF16)
            s.qkv[l, rows, D : 2 * D] = part[:, D : 2 * D].astype(BF16)
            s.qkv[l, rows, 2 * D :] = (part[:, 2 * D :] + s.vec[l, 3:4, :]).astype(BF16)
            return 0

        lax.fori_loop(0, BLOCKS, step, 0)
        s.o[l] = jnp.zeros((ROWS, D), BF16)

    def forward_attend(self, l, begin, end):
        s = self.s
        low = lax.broadcasted_iota(jnp.int32, (1, 128), 1) < HEAD_DIM

        def step(w, _):
            rows = pl.ds(window_start(w), WINDOW)
            bias = s.bias[w]
            for pair in range(HEADS // 2):
                base = pair * 128
                q = s.qkv[l, rows, base : base + 128]
                k = s.qkv[l, rows, D + base : D + base + 128]
                v = s.qkv[l, rows, 2 * D + base : 2 * D + base + 128]
                total = None
                for half in range(2):
                    keep = low if half == 0 else jnp.logical_not(low)
                    scores = dot_t(jnp.where(keep, k, jnp.zeros_like(k)), q) * (HEAD_DIM**-0.5) + bias
                    top = jnp.maximum(jnp.max(scores, axis=0, keepdims=True), -1e20)
                    weights = jnp.exp(scores - top)
                    summed = jnp.sum(weights, axis=0, keepdims=True)
                    weights = (weights * (1.0 / jnp.maximum(summed, 1e-20))).astype(BF16)
                    s.p[l, w, 2 * pair + half] = weights
                    part = t_dot(weights, jnp.where(keep, v, jnp.zeros_like(v)))
                    total = part if total is None else total + part
                old = s.o[l, rows, base : base + 128]
                s.o[l, rows, base : base + 128] = old + total.astype(BF16)
            return 0

        lax.fori_loop(begin, end, step, 0)

    def forward_second(self, l, u_ref, out_ref):
        s = self.s

        def step(i, _):
            rows = row_block(i)
            hidden = u_ref[rows, :].astype(F32) + dot(s.o[l, rows, :], load_proj(s.w, l)) + s.vec[l, 4:5, :]
            s.h[l, rows, :] = hidden
            normed, _unused = standard(hidden)
            c = (normed * s.vec[l, 5:6, :] + s.vec[l, 6:7, :]).astype(BF16)
            s.c[l, rows, :] = c
            total = hidden + s.vec[l, 7:8, :]
            for j in range(CHUNKS):
                cols = slice(j * CHUNK, (j + 1) * CHUNK)
                f = dot(c, load_up(s.w, l, j)) + s.bup[l, 0:1, cols]
                value, slope = gelu_pair(f)
                z = value.astype(BF16)
                s.z[l, rows, cols] = z
                s.slope[l, rows, cols] = slope.astype(BF16)
                total = total + dot(z, load_down(s.w, l, j))
            out_ref[rows, :] = total.astype(BF16)
            return 0

        lax.fori_loop(0, BLOCKS, step, 0)

    def backward_first(self, l, dy_ref):
        s = self.s
        s.gvec[l] = jnp.zeros_like(s.gvec[l])
        s.dbup[...] = jnp.zeros_like(s.dbup)

        def step(i, _):
            rows = row_block(i)
            dy = dy_ref[rows, :]
            dc = jnp.zeros((BLOCK, D), F32)
            for j in range(CHUNKS):
                cols = slice(j * CHUNK, (j + 1) * CHUNK)
                dz = dot_t(dy, load_down(s.w, l, j))
                df = (dz * s.slope[l, rows, cols].astype(F32)).astype(BF16)
                s.df[rows, cols] = df
                s.dbup[0:1, cols] += column_sum(df.astype(F32))
                dc = dc + dot_t(df, load_up(s.w, l, j))
            normed, inverse = standard(s.h[l, rows, :])
            top = dy.astype(F32)
            dh = top + norm_back(normed, inverse, s.vec[l, 5:6, :], dc)
            s.dh[rows, :] = dh
            dhb = dh.astype(BF16)
            s.dhb[rows, :] = dhb
            s.dout[rows, :] = dot_t(dhb, load_proj(s.w, l)).astype(BF16)
            s.gvec[l, 4:5, :] += column_sum(dhb.astype(F32))
            s.gvec[l, 5:6, :] += column_sum(dc * normed)
            s.gvec[l, 6:7, :] += column_sum(dc)
            s.gvec[l, 7:8, :] += column_sum(top)
            return 0

        lax.fori_loop(0, BLOCKS, step, 0)
        for j in range(FF // D):
            s.gvec[l, 8 + j : 9 + j, :] = s.dbup[0:1, j * D : (j + 1) * D]

    def grad_up(self, l):
        s = self.s
        for b in range(FF // D):
            value = t_dot(s.c[l], s.df[:, b * D : (b + 1) * D]).astype(BF16)
            store_rows(s.g, l, wide_tiles(up_tile, b), value)

    def grad_tall(self, l, dy_ref):
        s = self.s
        for b in range(FF // D):
            value = t_dot(s.z[l, :, b * D : (b + 1) * D], dy_ref[...]).astype(BF16)
            store_rows(s.g, l, tall_tiles(D + b * D, D), value)
        store_rows(s.g, l, tall_tiles(0, D), t_dot(s.o[l], s.dhb[...]).astype(BF16))

    def backward_attend(self, l, begin, end):
        s = self.s
        low = lax.broadcasted_iota(jnp.int32, (1, 128), 1) < HEAD_DIM

        def step(w, _):
            rows = pl.ds(window_start(w), WINDOW)
            for pair in range(HEADS // 2):
                base = pair * 128
                q = s.qkv[l, rows, base : base + 128]
                k = s.qkv[l, rows, D + base : D + base + 128]
                v = s.qkv[l, rows, 2 * D + base : 2 * D + base + 128]
                grad = s.dout[rows, base : base + 128]
                dq = dk = dv = None
                for half in range(2):
                    keep = low if half == 0 else jnp.logical_not(low)

                    def only(x, keep=keep):
                        return jnp.where(keep, x, jnp.zeros_like(x))

                    weights = s.p[l, w, 2 * pair + half]
                    grad_half = only(grad)
                    dv_part = dot(weights, grad_half)
                    dp = dot_t(v, grad_half)
                    wide_weights = weights.astype(F32)
                    product = dp * wide_weights
                    ds = (product - wide_weights * jnp.sum(product, axis=0, keepdims=True)).astype(BF16)
                    dk_part = dot(ds, only(q))
                    dq_part = t_dot(ds, only(k))
                    if half == 0:
                        dq, dk, dv = dq_part, dk_part, dv_part
                    else:
                        dq, dk, dv = dq + dq_part, dk + dk_part, dv + dv_part
                scale = HEAD_DIM**-0.5
                for offset, value in ((0, dq * scale), (D, dk * scale), (2 * D, dv)):
                    cols = slice(offset + base, offset + base + 128)
                    s.dqkv[rows, cols] = s.dqkv[rows, cols] + value.astype(BF16)
            return 0

        if begin == 0:
            s.dqkv[...] = jnp.zeros_like(s.dqkv)
        lax.fori_loop(begin, end, step, 0)

    def backward_last(self, l, u_ref, du_ref):
        s = self.s

        def step(i, _):
            rows = row_block(i)
            dqkv = s.dqkv[rows, :]
            da = dot_t(dqkv, load_qkv(s.w, l))
            normed, inverse = standard(u_ref[rows, :].astype(F32))
            du = s.dh[rows, :] + norm_back(normed, inverse, s.vec[l, 0:1, :], da)
            du_ref[rows, :] = du.astype(BF16)
            s.gvec[l, 0:1, :] += column_sum(da * normed)
            s.gvec[l, 1:2, :] += column_sum(da)
            s.gvec[l, 2:3, :] += column_sum(dqkv[:, 0:D].astype(F32))
            s.gvec[l, 3:4, :] += column_sum(dqkv[:, 2 * D : 3 * D].astype(F32))
            return 0

        lax.fori_loop(0, BLOCKS, step, 0)
        self.spread_gains(l)

    def grad_qkv(self, l):
        s = self.s
        for b in range(3):
            value = t_dot(s.a[l], s.dqkv[:, b * D : (b + 1) * D]).astype(BF16)
            store_rows(s.g, l, wide_tiles(qkv_tile, b), value)


COMPUTE = (
    ("w", (2, 4, 2, 2 * HALF, D), BF16),
    ("g", (2, 4, 2, 2 * HALF, D), BF16),
    ("vec", (2, TILE, D), F32),
    ("gvec", (2, TILE, D), F32),
    ("a", (2, ROWS, D), BF16),
    ("qkv", (2, ROWS, 3 * D), BF16),
    ("o", (2, ROWS, D), BF16),
    ("h", (2, ROWS, D), F32),
    ("c", (2, ROWS, D), BF16),
    ("z", (2, ROWS, FF), BF16),
    ("slope", (2, ROWS, FF), BF16),
    ("p", (2, WINDOWS, HEADS, WINDOW, WINDOW), BF16),
    ("bias", (WINDOWS, WINDOW, WINDOW), F32),
    ("bup", (2, 8, FF), F32),
    ("dbup", (8, FF), F32),
    ("df", (ROWS, FF), BF16),
    ("dh", (ROWS, D), F32),
    ("dhb", (ROWS, D), BF16),
    ("dout", (ROWS, D), BF16),
    ("dqkv", (ROWS, 3 * D), BF16),
)
LINKS = (
    ("near_wide", (24, 3 * D + FF), F32),
    ("near_tall", (120, D), F32),
    ("near_vec", (TILE, 128), F32),
    ("total", (2, HALF, D), F32),
    ("sum_x", (3, 7 * TILE, D), BF16),
    ("from_x", (3, 7 * TILE, D), BF16),
) + tuple(
    (f"{name}{l}{st}", (count, STAGES[st][1], D), BF16)
    for l in range(2)
    for st in range(3)
    for name, count in (("from_c", 8), ("from_y", 4), ("from_z", 3))
)


class Refs:
    pass


class Links:
    def __init__(self, s):
        self.s = s
        self.section = lax.axis_index("section")
        self.dp = lax.axis_index("dp")
        self.z, self.y, self.core = self.dp // 4, (self.dp // 2) % 2, self.dp % 2
        self.near = (self.section, self.dp + 1 - 2 * self.core)
        self.across = (1 - self.section, self.dp)
        self.beside = (self.section, self.dp + 2 - 4 * self.y)
        self.pending = []

    def level(self, steps):
        there = (self.z + steps) % 4
        return there, (self.section, self.dp + 4 * (there - self.z))

    def barrier(self):
        sem = pltpu.get_barrier_semaphore()
        others = [self.near, self.across, self.beside] + [self.level(i)[1] for i in (1, 2, 3)]
        for device in others:
            pl.semaphore_signal(sem, inc=1, device_id=device, device_id_type=MESH)
        pl.semaphore_wait(sem, len(others))

    def copy(self, src, dst, sems, index, device):
        return pltpu.make_async_remote_copy(
            src_ref=src,
            dst_ref=dst,
            send_sem=sems[0].at[index],
            recv_sem=sems[1].at[index],
            device_id=device,
            device_id_type=MESH,
        )

    def send(self, *args, when=None):
        made = self.copy(*args)
        if when is None:
            made.start()
        else:
            pl.when(when)(made.start)
        self.pending.append((made, when))

    def received(self, *args):
        self.copy(*args).wait_recv()

    def drain(self):
        for made, when in self.pending:
            if when is None:
                made.wait_send()
            else:
                pl.when(when)(made.wait_send)
        self.pending = []


    def near_start(self):
        s = self.s
        for index, (src, dst) in enumerate(
            ((s.wide_in, s.near_wide), (s.tall_in, s.near_tall), (s.vec_in, s.near_vec))
        ):
            self.send(src, dst, s.near_sems, index, self.near)

    def near_finish(self):
        s = self.s
        for index, (src, dst) in enumerate(
            ((s.wide_in, s.near_wide), (s.tall_in, s.near_tall), (s.vec_in, s.near_vec))
        ):
            self.received(src, dst, s.near_sems, index, self.near)
        first = self.core == 0

        def pair(own, near):
            return jnp.where(first, own, near), jnp.where(first, near, own)

        def put(tile, value):
            s.w[self.section, self.z, self.y, tile * TILE : (tile + 1) * TILE, :] = value

        rows = jnp.concatenate(pair(s.wide_in[...], s.near_wide[...]), axis=0).astype(BF16)
        for block in range(7):
            for i in range(3):
                tile = qkv_tile(3 * block + i) if block < 3 else up_tile(3 * (block - 3) + i)
                put(tile, rows[i * TILE : (i + 1) * TILE, block * D : (block + 1) * D])
        rows = jnp.concatenate(pair(s.tall_in[...], s.near_tall[...]), axis=0).astype(BF16)
        for i in range(15):
            put(tall_tile(i), rows[i * TILE : (i + 1) * TILE])
        for half, value in enumerate(pair(s.vec_in[...], s.near_vec[...])):
            put(vec_tile(half), jnp.concatenate((value, jnp.zeros((TILE, D - 128), F32)), axis=1).astype(BF16))

    def part(self, ref, l, z, y, stage, core):
        first, count = STAGES[stage]
        return ref.at[l, z, y, pl.ds(pl.multiple_of(core * HALF + first, TILE), count), :]

    def w_part(self, l, z, y, stage, core=None):
        return self.part(self.s.w, l, z, y, stage, self.core if core is None else core)

    def gather_across(self, l, stage):
        own = self.w_part(l, self.z, self.y, stage)
        self.send(own, own, self.s.w_sems, (l, stage, 0), self.across, when=self.section == l)

    def gather_begin(self, l, stage):
        s = self.s
        own = self.w_part(l, self.z, self.y, stage)

        @pl.when(self.section != l)
        def _():
            self.received(own, own, s.w_sems, (l, stage, 0), self.across)

        self.send(own, own, s.w_sems, (l, stage, 1), self.near, when=self.section != l)
        for i in (1, 2, 3):
            self.send(own, own, s.w_sems, (l, stage, 1 + i), self.level(i)[1])
        self.send(own, own, s.w_sems, (l, stage, 8), self.beside)

    def gather_z(self, l, stage):
        s = self.s
        for i in (1, 2, 3):
            came = self.w_part(l, self.level(4 - i)[0], self.y, stage)
            self.received(came, came, s.w_sems, (l, stage, 1 + i), self.level(i)[1])
            self.send(came, came, s.w_sems, (l, stage, 8 + i), self.beside)
            self.send(came, came, s.w_sems, (l, stage, 4 + i), self.near)

    def gather_y(self, l, stage):
        s = self.s
        for i in range(4):
            came = self.w_part(l, self.level(4 - i)[0], 1 - self.y, stage)
            self.received(came, came, s.w_sems, (l, stage, 8 + i), self.beside)
            self.send(came, came, s.w_sems, (l, stage, 12 + i), self.near)

    def gather_near(self, l, stage):
        s = self.s
        other = 1 - self.core
        own = self.w_part(l, self.z, self.y, stage, other)

        @pl.when(self.section != l)
        def _():
            self.received(own, own, s.w_sems, (l, stage, 1), self.near)

        for i in (1, 2, 3):
            came = self.w_part(l, self.level(4 - i)[0], self.y, stage, other)
            self.received(came, came, s.w_sems, (l, stage, 4 + i), self.near)
        for i in range(4):
            came = self.w_part(l, self.level(4 - i)[0], 1 - self.y, stage, other)
            self.received(came, came, s.w_sems, (l, stage, 12 + i), self.near)


    def rows_of(self, stage, core):
        first, count = STAGES[stage]
        return pl.ds(pl.multiple_of(core * HALF + first, TILE), count)

    def box(self, name, l, stage):
        return getattr(self.s, f"{name}{l}{stage}")

    def reduce_begin(self, l, stage):
        s = self.s
        for i in range(8):
            src = s.g.at[l, i // 2, i % 2, self.rows_of(stage, 1 - self.core), :]
            self.send(src, self.box("from_c", l, stage).at[i], s.c_sems, (l, stage, i), self.near)

    def reduce_near(self, l, stage):
        s = self.s
        box = self.box("from_c", l, stage)
        rows = self.rows_of(stage, self.core)
        for i in range(8):
            src = s.g.at[l, i // 2, i % 2, self.rows_of(stage, 1 - self.core), :]
            self.received(src, box.at[i], s.c_sems, (l, stage, i), self.near)

        def add(i, _):
            z, y = i // 2, i % 2
            s.g[l, z, y, rows, :] = (s.g[l, z, y, rows, :].astype(F32) + box[i].astype(F32)).astype(BF16)
            return 0

        lax.fori_loop(0, 8, add, 0)
        for i in range(4):
            self.send(
                s.g.at[l, i, 1 - self.y, rows, :], self.box("from_y", l, stage).at[i], s.g_sems, (l, stage, i), self.beside
            )

    def reduce_y(self, l, stage):
        s = self.s
        box = self.box("from_y", l, stage)
        rows = self.rows_of(stage, self.core)
        for i in range(4):
            self.received(s.g.at[l, i, 1 - self.y, rows, :], box.at[i], s.g_sems, (l, stage, i), self.beside)

        def add(i, _):
            s.g[l, i, self.y, rows, :] = (s.g[l, i, self.y, rows, :].astype(F32) + box[i].astype(F32)).astype(BF16)
            return 0

        lax.fori_loop(0, 4, add, 0)
        for i in (1, 2, 3):
            there, device = self.level(i)
            self.send(
                s.g.at[l, there, self.y, rows, :], self.box("from_z", l, stage).at[i - 1], s.g_sems, (l, stage, 3 + i), device
            )

    def reduce_z(self, l, stage):
        s = self.s
        box = self.box("from_z", l, stage)
        rows = self.rows_of(stage, self.core)
        count = STAGES[stage][1]
        for i in (1, 2, 3):
            there, device = self.level(i)
            self.received(s.g.at[l, there, self.y, rows, :], box.at[i - 1], s.g_sems, (l, stage, 3 + i), device)
        total = s.g[l, self.z, self.y, rows, :].astype(F32)
        for i in range(3):
            total = total + box[i].astype(F32)
        first = STAGES[stage][0]

        @pl.when(self.section == l)
        def _():
            s.total[self.core, first : first + count, :] = total

        @pl.when(self.section != l)
        def _():
            s.sum_x[stage, 0:count, :] = total.astype(BF16)

        self.send(
            s.sum_x.at[stage, 0:count, :],
            s.from_x.at[stage, 0:count, :],
            s.g_sems,
            (l, stage, 7),
            self.across,
            when=self.section != l,
        )

    def reduce_x(self, l, stage):
        s = self.s
        first, count = STAGES[stage]
        mine = s.total.at[self.core, first : first + count, :]

        @pl.when(self.section == l)
        def _():
            self.received(
                s.sum_x.at[stage, 0:count, :], s.from_x.at[stage, 0:count, :], s.g_sems, (l, stage, 7), self.across
            )
            mine[...] += s.from_x[stage, 0:count, :].astype(F32)

        self.send(mine, mine, s.g_sems, (l, stage, 8), self.near, when=self.section == l)

    def reduce_last(self, l, stage):
        s = self.s
        first, count = STAGES[stage]
        came = s.total.at[1 - self.core, first : first + count, :]

        @pl.when(self.section == l)
        def _():
            self.received(came, came, s.g_sems, (l, stage, 8), self.near)


def image_kernel(
    x, cot, wide_in, tall_in, vec_in, act, grads, far_act, far_grads, gwide, gtall, gvec_out, *scratch
):
    s = Refs()
    names = [name for name, _, _ in COMPUTE + LINKS] + ["near_sems", "w_sems", "c_sems", "g_sems", "o_sems"]
    flat = list(scratch)
    for name in names:
        if name.endswith("_sems"):
            setattr(s, name, (flat.pop(0), flat.pop(0)))
        else:
            setattr(s, name, flat.pop(0))
    s.wide_in, s.tall_in, s.vec_in = wide_in, tall_in, vec_in
    link, image = Links(s), Image(s)
    A, B, C = 0, 1, 2

    link.barrier()
    link.near_start()
    image.fill_bias()
    link.near_finish()
    for stage in (A, B, C):
        link.gather_across(0, stage)
        link.gather_across(1, stage)
    for stage in (A, B, C):
        link.gather_begin(0, stage)
    link.gather_z(0, A)
    link.gather_y(0, A)
    link.gather_z(0, B)
    link.gather_near(0, A)
    link.gather_begin(1, A)
    image.gains(0)
    image.forward_first(0, x)
    link.gather_y(0, B)
    image.forward_attend(0, 0, 2)
    link.gather_z(0, C)
    link.gather_begin(1, B)
    image.forward_attend(0, 2, WINDOWS)
    link.gather_y(0, C)
    link.gather_begin(1, C)
    link.gather_near(0, B)
    link.gather_near(0, C)
    link.gather_z(1, A)
    image.forward_second(0, x, act.at[0])
    out0 = (act.at[0], far_act, s.o_sems, 0, link.across)
    link.send(*out0, when=link.section == 1)
    link.gather_y(1, A)
    link.gather_z(1, B)
    link.gather_near(1, A)
    image.gains(1)
    image.forward_first(1, act.at[0])
    link.gather_y(1, B)
    image.forward_attend(1, 0, 2)
    link.gather_z(1, C)
    image.forward_attend(1, 2, WINDOWS)
    link.gather_y(1, C)
    link.gather_near(1, B)
    link.gather_near(1, C)
    image.forward_second(1, act.at[0], act.at[1])
    out1 = (act.at[1], far_act, s.o_sems, 0, link.across)
    link.send(*out1, when=link.section == 0)

    image.backward_first(1, cot)
    image.grad_up(1)
    link.reduce_begin(1, C)
    image.grad_tall(1, cot)
    link.reduce_near(1, C)
    link.reduce_begin(1, B)
    image.backward_attend(1, 0, 2)
    link.reduce_near(1, B)
    link.reduce_y(1, C)
    image.backward_attend(1, 2, WINDOWS)
    link.reduce_y(1, B)
    image.backward_last(1, act.at[0], grads.at[1])
    back1 = (grads.at[1], far_grads, s.o_sems, 1, link.across)
    link.send(*back1, when=link.section == 0)
    image.grad_qkv(1)
    link.reduce_begin(1, A)
    link.reduce_z(1, C)
    image.backward_first(0, grads.at[1])
    link.reduce_near(1, A)
    link.reduce_z(1, B)
    link.reduce_x(1, C)
    image.grad_up(0)
    link.reduce_begin(0, C)
    link.reduce_y(1, A)
    image.grad_tall(0, grads.at[1])
    link.reduce_near(0, C)
    link.reduce_begin(0, B)
    link.reduce_x(1, B)
    image.backward_attend(0, 0, 2)
    link.reduce_near(0, B)
    link.reduce_z(1, A)
    link.reduce_y(0, C)
    image.backward_attend(0, 2, WINDOWS)
    link.reduce_y(0, B)
    link.reduce_x(1, A)
    image.backward_last(0, x, grads.at[0])
    back0 = (grads.at[0], far_grads, s.o_sems, 1, link.across)
    link.send(*back0, when=link.section == 1)
    image.grad_qkv(0)
    link.reduce_begin(0, A)
    link.reduce_z(0, C)
    link.reduce_near(0, A)
    link.reduce_z(0, B)
    link.reduce_x(0, C)
    link.reduce_x(0, B)
    link.reduce_y(0, A)
    link.reduce_z(0, A)
    link.reduce_x(0, A)
    for l in range(2):
        for stage in (C, B, A):
            link.reduce_last(l, stage)

    first = link.core == 0
    for block in range(7):
        tiles = [
            qkv_tile(3 * block + i) if block < 3 else up_tile(3 * (block - 3) + i) for i in range(3)
        ]
        rows = jnp.concatenate(
            [s.total[t // 19, (t % 19) * TILE : (t % 19 + 1) * TILE, :] for t in tiles], axis=0
        )
        gwide[:, block * D : (block + 1) * D] = jnp.where(first, rows[0:24], rows[24:48])
    rows = jnp.concatenate(
        [
            s.total[tall_tile(i) // 19, (tall_tile(i) % 19) * TILE : (tall_tile(i) % 19 + 1) * TILE, :]
            for i in range(15)
        ],
        axis=0,
    )
    gtall[...] = jnp.where(first, rows[0:120], rows[120:240])
    at = (vec_tile(0) % 19) * TILE
    gvec_out[...] = jnp.where(first, s.total[0, at : at + TILE, 0:128], s.total[1, at : at + TILE, 0:128])

    link.received(*out0)
    link.received(*back0)
    link.drain()


def one_image(x, cot, wide, tall, vec):
    whole = pl.BlockSpec(memory_space=pltpu.VMEM)
    sems = [
        pltpu.SemaphoreType.DMA(shape)
        for shape in ((3,), (2, 3, 16), (2, 3, 8), (2, 3, 9), (2,))
        for _ in range(2)
    ]
    return pl.pallas_call(
        image_kernel,
        out_shape=(
            jax.ShapeDtypeStruct((2, ROWS, D), BF16),
            jax.ShapeDtypeStruct((2, ROWS, D), BF16),
            jax.ShapeDtypeStruct((ROWS, D), BF16),
            jax.ShapeDtypeStruct((ROWS, D), BF16),
            jax.ShapeDtypeStruct(wide.shape, F32),
            jax.ShapeDtypeStruct(tall.shape, F32),
            jax.ShapeDtypeStruct(vec.shape, F32),
        ),
        in_specs=[whole] * 5,
        out_specs=(whole,) * 7,
        scratch_shapes=[pltpu.VMEM(shape, dtype) for _, shape, dtype in COMPUTE + LINKS] + sems,
        compiler_params=pltpu.CompilerParams(
            vmem_limit_bytes=64 * 2**20, collective_id=0, has_side_effects=True
        ),
        cost_estimate=pl.CostEstimate(flops=18 * 10**9, bytes_accessed=20 * 10**6, transcendentals=10**7),
    )(x, cot, wide, tall, vec)


def adamw(weights, first, second, grads, rate, decay):
    first_new = BETA_ONE * first + (1.0 - BETA_ONE) * grads
    second_new = BETA_TWO * second + (1.0 - BETA_TWO) * grads * grads
    corrected = (
        first_new
        / (1.0 - BETA_ONE**STEP)
        / (jnp.sqrt(second_new / (1.0 - BETA_TWO**STEP)) + ADAM_EPS)
    )
    return (first_new, second_new, weights - rate * (corrected + decay * weights))


def plain_kernel(x, cot, w, act, grads, g, *scratch):
    s = Refs()
    s.w, s.g = w, g
    for (name, _, _), ref in zip(COMPUTE[2:], scratch):
        setattr(s, name, ref)
    image = Image(s)
    image.fill_bias()
    for l, u, out in ((0, x, act.at[0]), (1, act.at[0], act.at[1])):
        image.gains(l)
        image.forward_first(l, u)
        image.forward_attend(l, 0, WINDOWS)
        image.forward_second(l, u, out)
    for l, u, dy, du in ((1, act.at[0], cot, grads.at[1]), (0, x, grads.at[1], grads.at[0])):
        image.backward_first(l, dy)
        image.grad_up(l)
        image.grad_tall(l, dy)
        image.backward_attend(l, 0, WINDOWS)
        image.backward_last(l, u, du)
        image.grad_qkv(l)


def plain_image(x, cot, w):
    whole = pl.BlockSpec(memory_space=pltpu.VMEM)
    return pl.pallas_call(
        plain_kernel,
        out_shape=(
            jax.ShapeDtypeStruct((2, ROWS, D), BF16),
            jax.ShapeDtypeStruct((2, ROWS, D), BF16),
            jax.ShapeDtypeStruct(w.shape, BF16),
        ),
        in_specs=[whole] * 3,
        out_specs=(whole,) * 3,
        scratch_shapes=[pltpu.VMEM(shape, dtype) for _, shape, dtype in COMPUTE[2:]],
        compiler_params=pltpu.CompilerParams(vmem_limit_bytes=64 * 2**20),
    )(x, cot, w)


def tile_order():
    wide = [qkv_tile(i) for i in range(9)] + [up_tile(i) for i in range(12)]
    return wide + [tall_tile(i) for i in range(15)] + [vec_tile(half) for half in range(2)]


def any_mesh(
    inputs, cotangent, wide_weights, wide_first, wide_second, tall_weights, tall_first, tall_second,
    vectors, vector_first, vector_second,
):
    section = lax.axis_index("section")
    both = ("section", "dp")
    wide = lax.all_gather(wide_weights[0].astype(BF16), both, axis=0, tiled=True)
    tall = lax.all_gather(tall_weights[0].astype(BF16), both, axis=0, tiled=True)
    vec = lax.all_gather(lax.all_gather(vectors[0].astype(BF16), "dp", axis=1, tiled=True), "section", axis=0)
    vec_rows, width = vec.shape[1], D // (2 * SLOTS)
    order = tile_order()
    place = sorted(range(len(order)), key=order.__getitem__)
    wide = wide.reshape(2, SLOTS, 3, TILE, 7, D).transpose(0, 1, 4, 2, 3, 5).reshape(2, SLOTS, 21, TILE, D)
    tall = tall.reshape(2, SLOTS, 15, TILE, D)
    vec = vec.reshape(2, vec_rows, SLOTS, 2, width).transpose(0, 2, 3, 1, 4)
    vec = jnp.pad(vec, ((0, 0),) * 3 + ((0, TILE - vec_rows), (0, D - width)))
    tiles = jnp.concatenate((wide, tall, vec), axis=2)[:, :, jnp.array(place)]
    act, grads, g = plain_image(
        own_rows(inputs, section), own_rows(cotangent, section), tiles.reshape(2, SLOTS // 2, 2, 2 * HALF, D)
    )
    far_act, far_grads = (
        lax.ppermute(lax.dynamic_index_in_dim(array, 1 - section, keepdims=False), "section", [(0, 1), (1, 0)])
        for array in (act, grads)
    )
    g = g.reshape(2, SLOTS, len(order), TILE, D)[:, :, jnp.array(order)].astype(F32)
    wide = g[:, :, :21].reshape(2, SLOTS, 7, 3, TILE, D).transpose(0, 1, 3, 4, 2, 5).reshape(2, D, 7 * D)
    tall = g[:, :, 21:36].reshape(2, D + FF, D)
    vec = g[:, :, 36:, :vec_rows, :width].transpose(0, 3, 1, 2, 4).reshape(2, vec_rows, D)

    def reduced(array, dim):
        array = lax.psum_scatter(array, "section", scatter_dimension=0, tiled=False)
        return lax.psum_scatter(array, "dp", scatter_dimension=dim, tiled=True)

    return finish(
        section, act, grads, far_act, far_grads, reduced(wide, 0), reduced(tall, 0), reduced(vec, 1),
        wide_weights, wide_first, wide_second, tall_weights, tall_first, tall_second, vectors, vector_first, vector_second,
    )


def own_rows(array, section):
    return jnp.pad(lax.dynamic_slice_in_dim(array, section * IMG_TOK, IMG_TOK), ((0, ROWS - IMG_TOK), (0, 0)))


def finish(
    section, act, grads, far_act, far_grads, total_wide, total_tall, total_vec,
    wide_weights, wide_first, wide_second, tall_weights, tall_first, tall_second, vectors, vector_first, vector_second,
):
    def joined(array, other):
        mine = lax.dynamic_index_in_dim(array, section, keepdims=False)[:IMG_TOK]
        other = other[:IMG_TOK]
        return jnp.where(section == 0, jnp.concatenate((mine, other)), jnp.concatenate((other, mine)))

    wide_m, wide_s, wide_n = adamw(wide_weights[0], wide_first[0], wide_second[0], total_wide, RATE_MATRIX, DECAY)
    tall_m, tall_s, tall_n = adamw(tall_weights[0], tall_first[0], tall_second[0], total_tall, RATE_MATRIX, DECAY)
    vec_m, vec_s, vec_n = adamw(vectors[0], vector_first[0], vector_second[0], total_vec, RATE_VECTOR, 0.0)
    outs = (joined(act, far_act), joined(grads, far_grads), wide_m, wide_s, wide_n, tall_m, tall_s, tall_n, vec_m, vec_s, vec_n)
    return tuple(out[None] for out in outs)


def per_device(
    inputs, cotangent, wide_weights, wide_first, wide_second, tall_weights, tall_first, tall_second,
    vectors, vector_first, vector_second,
):
    section = lax.axis_index("section")
    rows, width = vectors.shape[1:]
    vec = jnp.pad(vectors[0], ((0, TILE - rows), (0, 128 - width)))
    act, grads, far_act, far_grads, total_wide, total_tall, total_vec = one_image(
        own_rows(inputs, section), own_rows(cotangent, section), wide_weights[0], tall_weights[0], vec
    )
    return finish(
        section, act, grads, far_act, far_grads, total_wide, total_tall, total_vec[:rows, :width],
        wide_weights, wide_first, wide_second, tall_weights, tall_first, tall_second, vectors, vector_first, vector_second,
    )


def solution(mesh):
    data = P("dp", None)
    matrix = P("section", "dp", None)
    vector = P("section", None, "dp")
    in_specs = (data, data) + (matrix,) * 6 + (vector,) * 3
    out_specs = (matrix,) * 8 + (vector,) * 3
    device_fn = per_device if mesh.shape["dp"] == 2 * SLOTS else any_mesh
    return jax.shard_map(device_fn, mesh=mesh, in_specs=in_specs, out_specs=out_specs, check_vma=False)
```

time: 456 us -> 184 us (0.40)
  waiting for transfers between devices: 257 us -> 0 us
  Pallas kernels: 73.6 us -> 169 us
  blocking collectives: 89.5 us -> 0 us
  between operations: 14.9 us -> 0.83 us
  other arithmetic: 11.2 us -> 4.82 us
    reduce_scatter x3 -> x0, waiting for transfers between devices: 103 us -> none  [the longest x2 94.7 us: reduced(): array = lax.psum_scatter(array, 'section', scatter_dimension=0, tiled=False)]
    pallas_call x1, Pallas kernels: 73.6 us -> 169 us  [one_image(): pl.pallas_call(image_kernel, out_shape=(jax.ShapeDtypeStruct((2, ROWS, D)...]
    all_gather x2 -> x0, waiting for transfers between devices: 94.6 us -> none  [the longest x1 63.9 us: per_device(): lax.all_gather(wide_weights[0].astype(BF16), both, axis=0, tiled=True)]
    unnamed x1 -> x0, blocking collectives: 61.9 us -> none
    unnamed x9 -> x0, waiting for transfers between devices: 59.4 us -> none
    all_gather x2 -> x0, blocking collectives: 27.6 us -> none  [the longest x1 23.2 us: per_device(): vec = lax.all_gather(vectors[0].astype(BF16), 'dp', axis=1, tiled=True)]
  transfers between devices with their start and end apart: 9 -> 0, of which waited for: 6 -> 0; matrix products, arithmetic and copies ran while one was open for 3% -> 0% of each run, Pallas kernels for 0% -> 0%
where the time goes in v2:
time: 184 us
  Pallas kernels  169 us (92%)
  local copies, waits for them, and re-layouts  8.54 us (5%)
  other arithmetic  4.82 us (3%)
    pallas_call x1, Pallas kernels, one_image(): pl.pallas_call(image_kernel, out_shape=(jax.ShapeDtypeStruct((2, ROWS, D)...  169 us

profile of v2, /device:TPU:0, one launch (start us, length us, event | category | flops | bytes accessed | tf_op | source)
XLA Modules:
  0.0 183.5 jit_solution(10125305115200323223)
XLA Ops:
  0.6 1.5 constant_dynamic-slice_fusion.2
  2.2 0.0 copy-start.11
  2.2 0.9 pad.11.x
  3.1 0.9 pad.12.cot
  4.0 0.6 pad.13.vec_in
  4.6 169.4 %shard_map.194 = (bf16[2,768,384]{2,1,0:T(8,128)(2,1)}, bf16[2,768,384]{2,1,0:T(8,128)(2,1)}, bf16[768,384]{1,0:T(8,128)(2,1)}, bf16[768,384]{1,0:T(8,128)(2,1)}...) custom-call(bf16[768,384]{1,0:T(8,128)(2,1)} %pad.11.x, bf16[768,384]{1,0:T(8,128)(2,1)} %pad.12.cot, ...), custom_call_target="tpu_custom_call" | custom-call | flops 17999998976 | bytes 20000000 | tf_op jit(solution)/shard_map/pallas_call | solution.py:847
  173.9 1.2 constant_dynamic-slice_fusion
  175.1 0.0 copy-done.1
  175.2 0.1 slice_bitcast_fusion
  175.3 1.4 maximum_select_fusion.1
  176.7 0.1 constant_dynamic-slice_fusion.1
  176.8 1.0 copy-done
  177.8 0.1 slice_bitcast_fusion.1
  177.8 0.0 copy-start.4
  177.9 0.0 copy-start.5
  177.9 1.5 maximum_select_fusion
  179.4 0.0 copy-start.12
  179.4 1.0 subtract_bitcast_fusion
  180.4 0.1 copy-done.9
  180.6 0.2 copy-done.10
  180.8 0.9 subtract_bitcast_fusion.1
  181.7 0.6 copy.24
  182.3 0.6 copy.25
  182.9 0.6 copy.26
  (26 shorter events, 0.1 us)
Async XLA Ops:
  2.2 1.8 copy-start.11
  173.9 1.2 copy-start.1
  175.2 1.5 copy-start.2
  176.7 1.1 copy-start
  177.8 1.5 copy-start.3
  177.8 1.5 copy-start.4
  177.9 1.5 copy-start.5
  177.9 1.5 copy-start.6
  179.3 1.1 copy-start.7
  179.3 1.1 copy-start.8
  179.3 1.2 copy-start.9
  179.3 1.5 copy-start.10
  179.4 2.3 %copy-start.12 = (f32[1,12,24]{2,0,1:T(1,128)S(1)}, f32[1,12,24]{2,0,1:T(1,128)}, u32[]{:S(2)}) copy-start(f32[1,12,24]{2,0,1:T(1,128)} %param.19) | copy-start | bytes 3460
  179.4 2.3 %copy-start.13 = (f32[16,128]{1,0:T(8,128)S(1)}, f32[16,128]{1,0:T(8,128)}, u32[]{:S(2)}) copy-start(f32[16,128]{1,0:T(8,128)} %get-tuple-element.24) | copy-start | bytes 24580
  179.4 2.3 %copy-start.14 = (f32[1,12,24]{2,0,1:T(1,128)S(1)}, f32[1,12,24]{2,0,1:T(1,128)}, u32[]{:S(2)}) copy-start(f32[1,12,24]{2,0,1:T(1,128)} %param.20) | copy-start | bytes 3460
  179.4 2.3 %copy-start.15 = (f32[1,12,24]{2,0,1:T(1,128)S(1)}, f32[1,12,24]{2,0,1:T(1,128)}, u32[]{:S(2)}) copy-start(f32[1,12,24]{2,0,1:T(1,128)} %param.21) | copy-start | bytes 3460
